TPU v7x, 128 devices: a whole 4x4x4 slice. The times are simulated.
128 devices in a mesh: grp: 4 (over x), dev: 32 (over y, z, core).
Axes of the slice: x: 4, y: 4, z: 4, core: 2. Of those that a mesh axis runs over, the one named last changes fastest.
Arguments:
- load: float32 [1024, 1024, 128], P('grp', 'dev'), may hold values from -11 to 11
- east_class: int32 [1024, 1024], P('grp', 'dev'), may hold values from 0 to 7
- north_class: int32 [1024, 1024], P('grp', 'dev'), may hold values from 0 to 7
- cond_table: float32 [8], replicated, may hold values from 0.25 to 4
- taps: int32 [128, 16], replicated, may hold values from 0 to 1048575
- tap_current: float32 [128, 16], replicated, may hold values from -16 to 16
Outputs:
- potential: float32 [1024, 1024, 128], P('grp', 'dev')
Inputs may be any that keep to these rules, and one draw needn't show every extreme that they name: `taps`: tap number i * 1024 + j stands for node (i, j).
All inputs are finite; a program needn't handle non-finite values.
Results may differ from a plain program's by a relative error of at most 0.0001.
Values sent between devices are 32-bit elements; how exact they have to be, the bound alone decides.
A program may use at most 128 MiB of HBM per device.

v0:
```python
import jax
import jax.numpy as jnp
from jax import lax
from jax.sharding import PartitionSpec as P

LEVELS = 5


RELAXATION = 0.8
SHUNT_CONDUCT = 0.01


def padded_2(shard, sides, width):
    edges = {}
    for axis, dim in sides:
        size, length = (lax.axis_size(axis), shard.shape[dim])
        up = [(i, (i + 1) % size) for i in range(size - 1)]
        last = lax.slice_in_dim(shard, length - width, length, axis=dim)
        first = lax.slice_in_dim(shard, 0, width, axis=dim)
        edges[dim] = (
            lax.ppermute(last, axis, up),
            lax.ppermute(first, axis, [(b, a) for a, b in up]),
        )
    done = []
    for _, dim in sides:
        low, high = edges[dim]
        around = [(width, width) if d in done else (0, 0) for d in range(shard.ndim)]
        shard = jnp.concatenate([jnp.pad(low, around), shard, jnp.pad(high, around)], axis=dim)
        done.append(dim)
    return shard


def with_halo(cells, sides, width):
    for axis, dim in sides:
        count = lax.axis_size(axis)
        ends = count - 1
        head = lax.slice_in_dim(cells, 0, width, axis=dim)
        tail = lax.slice_in_dim(cells, cells.shape[dim] - width, cells.shape[dim], axis=dim)
        cells = jnp.concatenate(
            [
                lax.ppermute(tail, axis, [(i, (i + 1) % count) for i in range(ends)]),
                cells,
                lax.ppermute(head, axis, [((i + 1) % count, i) for i in range(ends)]),
            ],
            axis=dim,
        )
    return cells


def shifted(shard, axis, by):
    size = lax.axis_size(axis)
    pairs = [(i, i + by) for i in range(size) if 0 <= i + by < size]
    return lax.ppermute(shard, axis, pairs)


def joined_along(pieces, dim):
    pieces = jnp.moveaxis(pieces, 0, dim)
    lengths = pieces.shape
    return pieces.reshape(*lengths[:dim], lengths[dim] * lengths[dim + 1], *lengths[dim + 2 :])


def copy_for_each(shard, axis):
    size = lax.axis_size(axis)
    return lax.all_to_all(
        jnp.broadcast_to(shard[None], (size, *shard.shape)), axis, 0, 0, tiled=True
    )


def gather_directly(shard, axis, dim):
    return joined_along(copy_for_each(shard, axis), dim)


def pad_diagonal(coef_pad, shunt):
    east_cond = coef_pad[0]
    north_cond = coef_pad[1]
    return (
        shunt
        + east_cond[1:-1, 1:-1]
        + east_cond[:-2, 1:-1]
        + north_cond[1:-1, 1:-1]
        + north_cond[1:-1, :-2]
    )


def operate_padded(padded, coef_pad, shunt):
    east_cond = coef_pad[0]
    north_cond = coef_pad[1]
    diagonal = pad_diagonal(coef_pad, shunt)
    applied = (
        diagonal[..., None] * padded[1:-1, 1:-1]
        - east_cond[1:-1, 1:-1, None] * padded[2:, 1:-1]
        - east_cond[:-2, 1:-1, None] * padded[:-2, 1:-1]
        - north_cond[1:-1, 1:-1, None] * padded[1:-1, 2:]
        - north_cond[1:-1, :-2, None] * padded[1:-1, :-2]
    )
    return (applied, diagonal)


def relax(padded, coef_pad, source, shunt):
    applied, diagonal = operate_padded(padded, coef_pad, shunt)
    return padded[1:-1, 1:-1] + RELAXATION * (source - applied) / diagonal[..., None]


def operate_lead(padded, coef_pad, shunt):
    east_cond = coef_pad[0]
    north_cond = coef_pad[1]
    diagonal = pad_diagonal(coef_pad, shunt)
    applied = (
        diagonal[None] * padded[:, 1:-1, 1:-1]
        - east_cond[None, 1:-1, 1:-1] * padded[:, 2:, 1:-1]
        - east_cond[None, :-2, 1:-1] * padded[:, :-2, 1:-1]
        - north_cond[None, 1:-1, 1:-1] * padded[:, 1:-1, 2:]
        - north_cond[None, 1:-1, :-2] * padded[:, 1:-1, :-2]
    )
    return (applied, diagonal)


def relax_lead(padded, coef_pad, source, shunt):
    applied, diagonal = operate_lead(padded, coef_pad, shunt)
    return padded[:, 1:-1, 1:-1] + RELAXATION * (source - applied) / diagonal[None]


def restrict(values):
    row_count, col_count, cand_count = values.shape
    return values.reshape(row_count // 2, 2, col_count // 2, 2, cand_count).sum(axis=(1, 3))


def restrict_lead(values):
    cand_count, row_count, col_count = values.shape
    return values.reshape(cand_count, row_count // 2, 2, col_count // 2, 2).sum(axis=(2, 4))


def prolong(values):
    return jnp.repeat(jnp.repeat(values, 2, axis=0), 2, axis=1)


def prolong_lead(values):
    return jnp.repeat(jnp.repeat(values, 2, axis=1), 2, axis=2)


def coarsen_conduct(conduct):
    pairs, row_count, col_count = conduct.shape
    coarse_east = conduct[0].reshape(row_count // 2, 2, col_count // 2, 2)[:, 1].sum(axis=-1)
    coarse_north = conduct[1].reshape(row_count // 2, 2, col_count // 2, 2)[:, :, :, 1].sum(axis=1)
    return jnp.stack([coarse_east, coarse_north])


def coarse_factor(east_cond, north_cond, shunt):
    row_count, col_count = east_cond.shape
    node_count = row_count * col_count
    west_cond = jnp.pad(east_cond, ((1, 0), (0, 0)))[:-1]
    south_cond = jnp.pad(north_cond, ((0, 0), (1, 0)))[:, :-1]
    diagonal = (shunt + east_cond + west_cond + north_cond + south_cond).reshape(-1)
    east_flat = east_cond.reshape(-1)
    north_flat = north_cond.reshape(-1)
    matrix = (
        jnp.diag(diagonal)
        - jnp.diag(east_flat[: node_count - col_count], col_count)
        - jnp.diag(east_flat[: node_count - col_count], -col_count)
        - jnp.diag(north_flat[: node_count - 1], 1)
        - jnp.diag(north_flat[: node_count - 1], -1)
    )
    return jnp.linalg.cholesky(matrix)


def space_rim(values):
    return padded_2(values, (("grp", 0), ("dev", 1)), 1)


def group_rim(values):
    padded = with_halo(values, (("grp", 1),), 1)
    return jnp.pad(padded, ((0, 0), (0, 0), (1, 1)))


def group_coef(conduct):
    from_below = shifted(conduct[:, -1:, :], "grp", 1)
    taller = jnp.concatenate([from_below, conduct, jnp.zeros_like(from_below)], axis=1)
    return jnp.pad(taller, ((0, 0), (0, 0), (1, 1)))


def body(load, east_class, north_class, cond_table, taps, tap_current):
    row_count, col_count, cand_count = load.shape
    row_start = lax.axis_index("grp") * row_count
    col_start = lax.axis_index("dev") * col_count
    all_rows = lax.axis_size("grp") * row_count
    all_cols = lax.axis_size("dev") * col_count
    class_ids = jnp.arange(cond_table.shape[0], dtype=jnp.int32)
    east_cond = jnp.sum(jnp.where(east_class[..., None] == class_ids, cond_table, 0.0), axis=-1)
    north_cond = jnp.sum(jnp.where(north_class[..., None] == class_ids, cond_table, 0.0), axis=-1)
    row_ids = row_start + jnp.arange(row_count, dtype=jnp.int32)
    col_ids = col_start + jnp.arange(col_count, dtype=jnp.int32)
    east_cond = jnp.where((row_ids < all_rows - 1)[:, None], east_cond, 0.0)
    north_cond = jnp.where((col_ids < all_cols - 1)[None, :], north_cond, 0.0)
    conduct = jnp.stack([east_cond, north_cond])
    tap_rows = taps // all_cols - row_start
    tap_cols = taps % all_cols - col_start
    row_hits = jnp.where(
        tap_rows[None] == jnp.arange(row_count, dtype=jnp.int32)[:, None, None],
        tap_current[None],
        0.0,
    )
    col_hits = (tap_cols[None] == jnp.arange(col_count, dtype=jnp.int32)[:, None, None]).astype(
        jnp.float32
    )
    injected = jnp.einsum("ick,jck->ijc", row_hits, col_hits, precision=lax.Precision.HIGHEST)
    source = injected - load
    switch = 4
    stored = []
    for height in range(LEVELS):
        shunt = SHUNT_CONDUCT * 4.0**height
        if height == switch:
            source = lax.all_to_all(
                jnp.moveaxis(source, 2, 0), "dev", split_axis=0, concat_axis=2, tiled=True
            )
            conduct = gather_directly(conduct, "dev", 2)
        if height < switch:
            coef_pad = with_halo(conduct, (("grp", 1), ("dev", 2)), 2)
            coef_thin = coef_pad[:, 1 : coef_pad.shape[1] - 1, 1 : coef_pad.shape[2] - 1]
            rhs_pad = padded_2(source, (("grp", 0), ("dev", 1)), 1)
            initial = RELAXATION * rhs_pad / pad_diagonal(coef_pad, shunt)[..., None]
            potential = relax(initial, coef_thin, source, shunt)
            applied = operate_padded(space_rim(potential), coef_thin, shunt)[0]
            stored.append((potential, source, rhs_pad, coef_pad, coef_thin))
            source = restrict(source - applied)
        else:
            coef_pad = group_coef(conduct)
            initial = RELAXATION * source / pad_diagonal(coef_pad, shunt)[None]
            potential = relax_lead(group_rim(initial), coef_pad, source, shunt)
            applied = operate_lead(group_rim(potential), coef_pad, shunt)[0]
            stored.append((potential, source, source, coef_pad, coef_pad))
            source = restrict_lead(source - applied)
        conduct = coarsen_conduct(conduct)
    whole_source, whole_conduct = (
        lax.all_gather(source, "grp", axis=1, tiled=True),
        lax.all_gather(conduct, "grp", axis=1, tiled=True),
    )
    factor = coarse_factor(whole_conduct[0], whole_conduct[1], SHUNT_CONDUCT * 4.0**LEVELS)
    cand_width, whole_rows, whole_cols = whole_source.shape
    solved = jax.scipy.linalg.cho_solve(
        (factor, True), whole_source.reshape(cand_width, whole_rows * whole_cols).T
    )
    solved = jnp.moveaxis(solved.reshape(whole_rows, whole_cols, cand_width), 2, 0)
    portion = source.shape[1]
    correction = lax.dynamic_slice_in_dim(solved, lax.axis_index("grp") * portion, portion, 1)
    for height in reversed(range(LEVELS)):
        shunt = SHUNT_CONDUCT * 4.0**height
        potential, source, rhs_pad, coef_pad, coef_thin = stored[height]
        if height < switch:
            potential = potential + prolong(correction)
            padded = with_halo(potential, (("grp", 0), ("dev", 1)), 2)
            middle = relax(padded, coef_pad, rhs_pad, shunt)
            potential = relax(middle, coef_thin, source, shunt)
        else:
            potential = potential + prolong_lead(correction)
            for iteration in range(2):
                potential = relax_lead(group_rim(potential), coef_pad, source, shunt)
            potential = jnp.moveaxis(
                lax.all_to_all(potential, "dev", split_axis=2, concat_axis=0, tiled=True), 0, 2
            )
        correction = potential
    return correction


def solution(mesh):
    return jax.shard_map(
        body,
        mesh=mesh,
        in_specs=(P("grp", "dev", None), P("grp", "dev"), P("grp", "dev"), P(), P(), P()),
        out_specs=P("grp", "dev", None),
        check_vma=False,
    )
```

profile of v0, /device:TPU:8, one launch (start us, length us, event | category | flops | bytes accessed | tf_op | source)
XLA Modules:
  0.0 924.7 jit_solution(9872614775119093043)
XLA Ops:
  26.7 8.6 all-to-all-start.1
  122.5 11.9 %all_gather.6 = f32[2,32,32]{2,1,0:T(8,128)S(1)} all-gather(f32[2,8,32]{2,1,0:T(8,128)S(1)} %pad_maximum_fusion.77), channel_id=1, replica_groups=mesh['grp'=4,'dev'=32] {'grp'}, dimensions={1}, use_global_device_ids=true | all-gather | bytes 10240 | tf_op jit(solution)/shard_map/all_gather | solution.py:235
  142.6 11.7 %cholesky.222 = f32[128,128]{1,0:T(8,128)S(1)} custom-call(f32[128,128]{1,0:T(8,128)S(1)} %cholesky.577), custom_call_target="Cholesky" | custom-call | tf_op jit(solution)/shard_map/jit(cholesky)/cholesky | solution.py:163
  161.2 9.8 %custom-call.66 = f32[1,128,128]{1,2,0:T(8,128)S(1)} custom-call(f32[1,128,128]{2,1,0:T(8,128)S(1)} %get-tuple-element.100), custom_call_target="InvertDiagBlocksLowerTriangular" | custom-call | tf_op jit(solution)/shard_map/jit(cholesky)/cholesky | solution.py:163
  175.0 11.7 %cholesky.243 = f32[128,128]{1,0:T(8,128)S(1)} custom-call(f32[128,128]{1,0:T(8,128)S(1)} %cholesky.581), custom_call_target="Cholesky" | custom-call | tf_op jit(solution)/shard_map/jit(cholesky)/cholesky | solution.py:163
  188.0 9.8 %custom-call.67 = f32[1,128,128]{1,2,0:T(8,128)S(1)} custom-call(f32[1,128,128]{2,1,0:T(8,128)S(1)} %get-tuple-element.97), custom_call_target="InvertDiagBlocksLowerTriangular" | custom-call | tf_op jit(solution)/shard_map/jit(cholesky)/cholesky | solution.py:163
  201.2 11.9 %cholesky.466 = f32[128,128]{1,0:T(8,128)S(1)} custom-call(f32[128,128]{1,0:T(8,128)S(1)} %cholesky.586), custom_call_target="Cholesky" | custom-call | tf_op jit(solution)/shard_map/jit(cholesky)/cholesky | solution.py:163
  213.7 9.8 %custom-call.68 = f32[1,128,128]{1,2,0:T(8,128)S(1)} custom-call(f32[1,128,128]{2,1,0:T(8,128)S(1)} %get-tuple-element.94), custom_call_target="InvertDiagBlocksLowerTriangular" | custom-call | tf_op jit(solution)/shard_map/jit(cholesky)/cholesky | solution.py:163
  227.0 11.7 %cholesky.485 = f32[128,128]{1,0:T(8,128)S(1)} custom-call(f32[128,128]{1,0:T(8,128)S(1)} %cholesky.591), custom_call_target="Cholesky" | custom-call | tf_op jit(solution)/shard_map/jit(cholesky)/cholesky | solution.py:163
  239.4 9.8 %custom-call.69 = f32[1,128,128]{1,2,0:T(8,128)S(1)} custom-call(f32[1,128,128]{2,1,0:T(8,128)S(1)} %get-tuple-element.91), custom_call_target="InvertDiagBlocksLowerTriangular" | custom-call | tf_op jit(solution)/shard_map/jit(cholesky)/cholesky | solution.py:163
  252.9 11.7 %cholesky.504 = f32[128,128]{1,0:T(8,128)S(1)} custom-call(f32[128,128]{1,0:T(8,128)S(1)} %cholesky.596), custom_call_target="Cholesky" | custom-call | tf_op jit(solution)/shard_map/jit(cholesky)/cholesky | solution.py:163
  265.8 9.8 %custom-call.70 = f32[1,128,128]{1,2,0:T(8,128)S(1)} custom-call(f32[1,128,128]{2,1,0:T(8,128)S(1)} %get-tuple-element.88), custom_call_target="InvertDiagBlocksLowerTriangular" | custom-call | tf_op jit(solution)/shard_map/jit(cholesky)/cholesky | solution.py:163
  278.9 12.0 %cholesky.524 = f32[128,128]{1,0:T(8,128)S(1)} custom-call(f32[128,128]{1,0:T(8,128)S(1)} %cholesky.601), custom_call_target="Cholesky" | custom-call | tf_op jit(solution)/shard_map/jit(cholesky)/cholesky | solution.py:163
  291.6 9.8 %custom-call.71 = f32[1,128,128]{1,2,0:T(8,128)S(1)} custom-call(f32[1,128,128]{2,1,0:T(8,128)S(1)} %get-tuple-element.85), custom_call_target="InvertDiagBlocksLowerTriangular" | custom-call | tf_op jit(solution)/shard_map/jit(cholesky)/cholesky | solution.py:163
  304.4 11.7 %cholesky.544 = f32[128,128]{1,0:T(8,128)S(1)} custom-call(f32[128,128]{1,0:T(8,128)S(1)} %cholesky.606), custom_call_target="Cholesky" | custom-call | tf_op jit(solution)/shard_map/jit(cholesky)/cholesky | solution.py:163
  317.3 9.8 %custom-call.72 = f32[1,128,128]{1,2,0:T(8,128)S(1)} custom-call(f32[1,128,128]{2,1,0:T(8,128)S(1)} %get-tuple-element.82), custom_call_target="InvertDiagBlocksLowerTriangular" | custom-call | tf_op jit(solution)/shard_map/jit(cholesky)/cholesky | solution.py:163
  329.7 11.9 %cholesky.562 = f32[128,128]{1,0:T(8,128)S(1)} custom-call(f32[128,128]{1,0:T(8,128)S(1)} %convolution_subtract_fusion.6), custom_call_target="Cholesky" | custom-call | tf_op jit(solution)/shard_map/jit(cholesky)/cholesky | solution.py:163
  350.0 7.1 multiply_divide_fusion
  389.6 15.9 %fusion.21 = f32[256,32,128]{0,1,2:T(8,128)} fusion(f32[256,32,128]{0,1,2:T(8,128)} %copy-done, f32[256,1,128]{0,1,2:T(1,128)S(1)} %collective-permute-done.11, f32[1,32,128]{0,1,2:T(8,128)} %copy.404, f32[256,32,128]{0,1,2:T(8,128)} %fusion.33, f32[1,32,128]{0,1,2:T(8,128)S(1)} %copy.406, f32[256,1,128]{0,1,2:T(1,128)S(1)} %collective-permute-done.10, ...), kind=kLoop, calls=%fused_computation.43 | loop fusion | flops 25165824 | bytes 13041664 | tf_op jit(solution)/shard_map/sub | solution.py:224
  566.5 28.4 %while.1 = (s32[]{:T(128)}, f32[1024,1024]{1,0:T(8,128)}, s32[8,2]{0,1:T(2,128)S(1)}, f32[8,128,128]{2,1,0:T(8,128)}, s32[]{:T(128)}) while((s32[]{:T(128)}, f32[1024,1024]{1,0:T(8,128)}, s32[8,2]{0,1:T(2,128)S(1)}, f32[8,128,128]{2,1,0:T(8,128)}, s32[]{:T(128)}) %tuple.147), condition=%wide.while_cond, body=%wide.while_body.sunk | while | flops 2 | bytes 132205 | solution.py:239
  594.9 80.0 %custom-call.73 = f32[8,128,128]{1,2,0:T(8,128)} custom-call(f32[8,128,128]{2,1,0:T(8,128)} %get-tuple-element.12), custom_call_target="InvertDiagBlocksLowerTriangular" | custom-call | tf_op jit(solution)/shard_map/jit(_cho_solve)/triangular_solve | solution.py:239
  680.8 13.3 %all_gather.7 = f32[4,32,32]{2,0,1:T(4,128)S(1)} all-gather(f32[4,8,32]{2,0,1:T(4,128)S(1)} %copy.444), channel_id=1, replica_groups=mesh['grp'=4,'dev'=32] {'grp'}, dimensions={1}, use_global_device_ids=true | all-gather | bytes 20480 | tf_op jit(solution)/shard_map/all_gather | solution.py:234
  750.4 10.7 %all_to_all.41 = f32[32,1,128]{2,1,0:T(1,128)S(1)} all-to-all(f32[32,1,128]{2,1,0:T(1,128)S(1)} %reshape.338), channel_id=1, replica_groups=mesh['grp'=4,'dev'=32] {'dev'}, dimensions={0} | all-to-all | bytes 32768 | tf_op jit(solution)/shard_map/all_to_all | solution.py:258
  887.0 24.7 %fusion.5 = f32[258,34,128]{0,1,2:T(8,128)S(1)} fusion(f32[260,2,128]{0,1,2:T(2,128)S(1)} %collective-permute-done.71, f32[2,32,128]{0,1,2:T(8,128)} %copy.470, f32[256,32,128]{0,1,2:T(8,128)} %copy-done.3, f32[2,32,128]{0,1,2:T(8,128)} %copy-done.5, f32[260,2,128]{0,1,2:T(2,128)S(1)} %collective-permute-done.72, f32[260,36,128]{0,1,2:T(8,128)S(1)} %pad_maximum_fusion.6, ...), kind=kLoop, calls=%fused_computation.8 | loop fusion | flops 30316032 | bytes 27422032 | tf_op jit(solution)/shard_map/add | solution.py:101
  (639 shorter events, 581.3 us)
Async XLA Ops:
  1.2 72.6 %collective-permute-start.4 = (f32[2,2,32]{1,2,0:T(8,128)S(1)}, f32[2,2,32]{1,2,0:T(8,128)S(1)}, u32[]{:S(2)}, u32[]{:S(2)}) collective-permute-start(f32[2,2,32]{1,2,0:T(8,128)S(1)} %get-tuple-element.109), channel_id=1, source_target_pairs={{0,32},{32,64},{64,96},{1,33},{33,65},{65,97},{2,34},{34,66},{66,9... | collective-permute-start | bytes 1544 | tf_op jit(solution)/shard_map/ppermute | solution.py:41
  4.6 71.1 %collective-permute-start.5 = (f32[2,2,32]{1,2,0:T(8,128)S(1)}, f32[2,2,32]{1,2,0:T(8,128)S(1)}, u32[]{:S(2)}, u32[]{:S(2)}) collective-permute-start(f32[2,2,32]{1,2,0:T(8,128)S(1)} %get-tuple-element.110), channel_id=1, source_target_pairs={{32,0},{64,32},{96,64},{33,1},{65,33},{97,65},{34,2},{66,34},{98,6... | collective-permute-start | bytes 1544 | tf_op jit(solution)/shard_map/ppermute | solution.py:43
  14.3 52.4 %collective-permute-start.16 = (f32[2,2,16]{1,2,0:T(8,128)S(1)}, f32[2,2,16]{1,2,0:T(8,128)S(1)}, u32[]{:S(2)}, u32[]{:S(2)}) collective-permute-start(f32[2,2,16]{1,2,0:T(8,128)S(1)} %get-tuple-element.150), channel_id=1, source_target_pairs={{0,32},{32,64},{64,96},{1,33},{33,65},{65,97},{2,34},{34,66},{66,9... | collective-permute-start | bytes 776 | tf_op jit(solution)/shard_map/ppermute | solution.py:41
  20.9 33.6 %collective-permute-start.40 = (f32[2,2,4]{1,2,0:T(4,128)S(1)}, f32[2,2,4]{1,2,0:T(4,128)S(1)}, u32[]{:S(2)}, u32[]{:S(2)}) collective-permute-start(f32[2,2,4]{1,2,0:T(4,128)S(1)} %get-tuple-element.189), channel_id=1, source_target_pairs={{0,32},{32,64},{64,96},{1,33},{33,65},{65,97},{2,34},{34,66},{66,9... | collective-permute-start | bytes 200 | tf_op jit(solution)/shard_map/ppermute | solution.py:41
  24.3 34.8 %collective-permute-start.41 = (f32[2,2,4]{1,2,0:T(4,128)S(1)}, f32[2,2,4]{1,2,0:T(4,128)S(1)}, u32[]{:S(2)}, u32[]{:S(2)}) collective-permute-start(f32[2,2,4]{1,2,0:T(4,128)S(1)} %get-tuple-element.190), channel_id=1, source_target_pairs={{32,0},{64,32},{96,64},{33,1},{65,33},{97,65},{34,2},{66,34},{98,6... | collective-permute-start | bytes 200 | tf_op jit(solution)/shard_map/ppermute | solution.py:43
  26.7 95.6 %all-to-all-start.1 = ((f32[32,2,16,2]{2,3,1,0:T(2,128)}), f32[32,2,16,2]{2,3,1,0:T(2,128)S(1)}, u32[]{:S(2)}, u32[]{:S(2)}) async-start(f32[32,2,16,2]{2,3,1,0:T(2,128)} %broadcast_in_dim.164), calls=%async_computation.1 | async-start | bytes 131072 | tf_op jit(solution)/shard_map/all_to_all | solution.py:64
  64.6 285.3 %collective-permute-start = (f32[256,1,128]{0,1,2:T(1,128)S(1)}, f32[256,1,128]{0,1,2:T(1,128)S(1)}, u32[]{:S(2)}, u32[]{:S(2)}) collective-permute-start(f32[256,1,128]{0,1,2:T(1,128)S(1)} %get-tuple-element.33), channel_id=1, source_target_pairs={{0,1},{1,2},{2,3},{3,4},{4,5},{5,6},{6,7},{7,8},{8,9},{9,10},{10,1... | collective-permute-start | bytes 393224 | tf_op jit(solution)/shard_map/ppermute | solution.py:21
  66.6 283.3 %collective-permute-start.3 = (f32[256,1,128]{0,1,2:T(1,128)S(1)}, f32[256,1,128]{0,1,2:T(1,128)S(1)}, u32[]{:S(2)}, u32[]{:S(2)}) collective-permute-start(f32[256,1,128]{0,1,2:T(1,128)S(1)} %get-tuple-element.34), channel_id=1, source_target_pairs={{1,0},{2,1},{3,2},{4,3},{5,4},{6,5},{7,6},{8,7},{9,8},{10,9},{11,1... | collective-permute-start | bytes 393224 | tf_op jit(solution)/shard_map/ppermute | solution.py:22
  72.4 274.7 %collective-permute-start.2 = (f32[1,32,128]{2,1,0:T(8,128)S(1)}, f32[1,32,128]{2,1,0:T(8,128)S(1)}, u32[]{:S(2)}, u32[]{:S(2)}) collective-permute-start(f32[1,32,128]{2,1,0:T(8,128)S(1)} %copy.400), channel_id=1, source_target_pairs={{32,0},{64,32},{96,64},{33,1},{65,33},{97,65},{34,2},{66,34},{98,6... | collective-permute-start | bytes 49160 | tf_op jit(solution)/shard_map/ppermute | solution.py:22
  93.7 12.8 %collective-permute-start.18 = (f32[2,132,2]{1,2,0:T(2,128)S(1)}, f32[2,132,2]{1,2,0:T(2,128)S(1)}, u32[]{:S(2)}, u32[]{:S(2)}) collective-permute-start(f32[2,132,2]{1,2,0:T(2,128)S(1)} %get-tuple-element.125), channel_id=1, source_target_pairs={{0,1},{1,2},{2,3},{3,4},{4,5},{5,6},{6,7},{7,8},{8,9},{9,10},{10,1... | collective-permute-start | bytes 6344 | tf_op jit(solution)/shard_map/ppermute | solution.py:41
  95.7 12.8 %collective-permute-start.19 = (f32[2,132,2]{1,2,0:T(2,128)S(1)}, f32[2,132,2]{1,2,0:T(2,128)S(1)}, u32[]{:S(2)}, u32[]{:S(2)}) collective-permute-start(f32[2,132,2]{1,2,0:T(2,128)S(1)} %get-tuple-element.126), channel_id=1, source_target_pairs={{1,0},{2,1},{3,2},{4,3},{5,4},{6,5},{7,6},{8,7},{9,8},{10,9},{11,1... | collective-permute-start | bytes 6344 | tf_op jit(solution)/shard_map/ppermute | solution.py:43
  116.0 228.2 %collective-permute-start.1 = (f32[1,32,128]{2,1,0:T(8,128)S(1)}, f32[1,32,128]{2,1,0:T(8,128)S(1)}, u32[]{:S(2)}, u32[]{:S(2)}) collective-permute-start(f32[1,32,128]{2,1,0:T(8,128)S(1)} %copy.399), channel_id=1, source_target_pairs={{0,32},{32,64},{64,96},{1,33},{33,65},{65,97},{2,34},{34,66},{66,9... | collective-permute-start | bytes 49160 | tf_op jit(solution)/shard_map/ppermute | solution.py:21
  157.6 321.4 %collective-permute-start.48 = (f32[2,1,64]{1,2,0:T(8,128)}, f32[2,1,64]{1,2,0:T(8,128)}, u32[]{:S(2)}, u32[]{:S(2)}) collective-permute-start(f32[2,1,64]{1,2,0:T(8,128)} %slice.1687), channel_id=1, source_target_pairs={{0,32},{32,64},{64,96},{1,33},{33,65},{65,97},{2,34},{34,66},{66,9... | collective-permute-start | bytes 1544 | tf_op jit(solution)/shard_map/ppermute | solution.py:53
  364.8 24.8 %collective-permute-start.10 = (f32[256,1,128]{0,1,2:T(1,128)S(1)}, f32[256,1,128]{0,1,2:T(1,128)S(1)}, u32[]{:S(2)}, u32[]{:S(2)}) collective-permute-start(f32[256,1,128]{0,1,2:T(1,128)S(1)} %get-tuple-element.29), channel_id=1, source_target_pairs={{1,0},{2,1},{3,2},{4,3},{5,4},{6,5},{7,6},{8,7},{9,8},{10,9},{11,1... | collective-permute-start | bytes 393224 | tf_op jit(solution)/shard_map/ppermute | solution.py:22
  366.7 22.9 %collective-permute-start.11 = (f32[256,1,128]{0,1,2:T(1,128)S(1)}, f32[256,1,128]{0,1,2:T(1,128)S(1)}, u32[]{:S(2)}, u32[]{:S(2)}) collective-permute-start(f32[256,1,128]{0,1,2:T(1,128)S(1)} %get-tuple-element.30), channel_id=1, source_target_pairs={{0,1},{1,2},{2,3},{3,4},{4,5},{5,6},{6,7},{7,8},{8,9},{9,10},{10,1... | collective-permute-start | bytes 393224 | tf_op jit(solution)/shard_map/ppermute | solution.py:21
  417.3 14.3 %collective-permute-start.13 = (f32[1,16,128]{2,1,0:T(8,128)S(1)}, f32[1,16,128]{2,1,0:T(8,128)S(1)}, u32[]{:S(2)}, u32[]{:S(2)}) collective-permute-start(f32[1,16,128]{2,1,0:T(8,128)S(1)} %get-tuple-element.47), channel_id=1, source_target_pairs={{0,32},{32,64},{64,96},{1,33},{33,65},{65,97},{2,34},{34,66},{66,9... | collective-permute-start | bytes 24584 | tf_op jit(solution)/shard_map/ppermute | solution.py:21
  436.0 13.9 %collective-permute-start.21 = (f32[1,16,128]{2,1,0:T(8,128)S(1)}, f32[1,16,128]{2,1,0:T(8,128)S(1)}, u32[]{:S(2)}, u32[]{:S(2)}) collective-permute-start(f32[1,16,128]{2,1,0:T(8,128)S(1)} %get-tuple-element.43), channel_id=1, source_target_pairs={{0,32},{32,64},{64,96},{1,33},{33,65},{65,97},{2,34},{34,66},{66,9... | collective-permute-start | bytes 24584 | tf_op jit(solution)/shard_map/ppermute | solution.py:21
  460.0 20.0 %collective-permute-start.25 = (f32[1,8,128]{2,1,0:T(8,128)S(1)}, f32[1,8,128]{2,1,0:T(8,128)S(1)}, u32[]{:S(2)}, u32[]{:S(2)}) collective-permute-start(f32[1,8,128]{2,1,0:T(8,128)S(1)} %get-tuple-element.59), channel_id=1, source_target_pairs={{0,32},{32,64},{64,96},{1,33},{33,65},{65,97},{2,34},{34,66},{66,9... | collective-permute-start | bytes 12296 | tf_op jit(solution)/shard_map/ppermute | solution.py:21
  464.3 15.7 %collective-permute-start.26 = (f32[1,8,128]{2,1,0:T(8,128)S(1)}, f32[1,8,128]{2,1,0:T(8,128)S(1)}, u32[]{:S(2)}, u32[]{:S(2)}) collective-permute-start(f32[1,8,128]{2,1,0:T(8,128)S(1)} %get-tuple-element.60), channel_id=1, source_target_pairs={{32,0},{64,32},{96,64},{33,1},{65,33},{97,65},{34,2},{66,34},{98,6... | collective-permute-start | bytes 12296 | tf_op jit(solution)/shard_map/ppermute | solution.py:22
  465.6 14.4 %collective-permute-start.24 = (f32[64,1,128]{2,1,0:T(1,128)S(1)}, f32[64,1,128]{2,1,0:T(1,128)S(1)}, u32[]{:S(2)}, u32[]{:S(2)}) collective-permute-start(f32[64,1,128]{2,1,0:T(1,128)S(1)} %get-tuple-element.57), channel_id=1, source_target_pairs={{0,1},{1,2},{2,3},{3,4},{4,5},{5,6},{6,7},{7,8},{8,9},{9,10},{10,1... | collective-permute-start | bytes 98312 | tf_op jit(solution)/shard_map/ppermute | solution.py:21
  496.6 13.6 %collective-permute-start.37 = (f32[1,4,128]{2,1,0:T(4,128)S(1)}, f32[1,4,128]{2,1,0:T(4,128)S(1)}, u32[]{:S(2)}, u32[]{:S(2)}) collective-permute-start(f32[1,4,128]{2,1,0:T(4,128)S(1)} %get-tuple-element.107), channel_id=1, source_target_pairs={{0,32},{32,64},{64,96},{1,33},{33,65},{65,97},{2,34},{34,66},{66,9... | collective-permute-start | bytes 6152 | tf_op jit(solution)/shard_map/ppermute | solution.py:21
  513.5 13.3 %collective-permute-start.45 = (f32[1,4,128]{2,1,0:T(4,128)S(1)}, f32[1,4,128]{2,1,0:T(4,128)S(1)}, u32[]{:S(2)}, u32[]{:S(2)}) collective-permute-start(f32[1,4,128]{2,1,0:T(4,128)S(1)} %get-tuple-element.103), channel_id=1, source_target_pairs={{0,32},{32,64},{64,96},{1,33},{33,65},{65,97},{2,34},{34,66},{66,9... | collective-permute-start | bytes 6152 | tf_op jit(solution)/shard_map/ppermute | solution.py:21
  560.6 114.3 %collective-permute-start.52 = (f32[4,1,64]{1,2,0:T(8,128)S(1)}, f32[4,1,64]{1,2,0:T(8,128)S(1)}, u32[]{:S(2)}, u32[]{:S(2)}) collective-permute-start(f32[4,1,64]{1,2,0:T(8,128)S(1)} %get-tuple-element.65), channel_id=1, source_target_pairs={{0,32},{32,64},{64,96},{1,33},{33,65},{65,97},{2,34},{34,66},{66,9... | collective-permute-start | bytes 3080 | tf_op jit(solution)/shard_map/ppermute | solution.py:41
  565.2 109.7 %collective-permute-start.51 = (f32[4,1,64]{1,2,0:T(8,128)S(1)}, f32[4,1,64]{1,2,0:T(8,128)}, u32[]{:S(2)}, u32[]{:S(2)}) collective-permute-start(f32[4,1,64]{1,2,0:T(8,128)S(1)} %get-tuple-element.66), channel_id=1, source_target_pairs={{32,0},{64,32},{96,64},{33,1},{65,33},{97,65},{34,2},{66,34},{98,6... | collective-permute-start | bytes 3080 | tf_op jit(solution)/shard_map/ppermute | solution.py:43
  (116 other events, 3572.6 us)
where the time goes:
time: 939 us; the launch traced here: 925 us
  other arithmetic  385 us (41%)
  starting transfers between devices  224 us (24%)
  local copies, waits for them, and re-layouts  141 us (15%)
  waiting for transfers between devices  67.6 us (7%)
  matrix products  62.8 us (7%)
  blocking collectives  35.9 us (4%)
    another operation x31, other arithmetic, coarse_factor(): return jnp.linalg.cholesky(matrix)  175 us
    another operation x3, other arithmetic, body(): jax.scipy.linalg.cho_solve((factor, True), whole_source.reshape(cand_widt...  85.4 us
    ppermute x20, starting transfers between devices, with_halo(): lax.ppermute(tail, axis, [(i, (i + 1) % count) for i in range(ends)])  58.8 us
    ppermute x16, starting transfers between devices, padded_2(): lax.ppermute(last, axis, up)  52.3 us
    add x12, other arithmetic, relax(): padded[1:-1, 1:-1] + RELAXATION * (source - applied) / diagonal[..., None]  51.7 us
    ppermute x16, starting transfers between devices, padded_2(): lax.ppermute(first, axis, [(b, a) for a, b in up])  48.6 us
    ppermute x20, starting transfers between devices, with_halo(): lax.ppermute(head, axis, [((i + 1) % count, i) for i in range(ends)])  47.9 us
    another operation x30, matrix products, body(): jax.scipy.linalg.cho_solve((factor, True), whole_source.reshape(cand_widt...  34 us
  transfers between devices with their start and end apart: 75, of which 23 were waited for; matrix products, arithmetic and copies ran while one was open for 49% of the time, Pallas kernels for 0%

commit v1 on v0

v1 whole, which is shorter than its diff:
```python
import functools

import jax
import jax.numpy as jnp
from jax import lax
from jax.experimental import pallas as pl
from jax.experimental.pallas import tpu as pltpu
from jax.sharding import PartitionSpec as P

MESH = pl.DeviceIdType.MESH
HI = lax.Precision.HIGHEST
F32 = jnp.float32
LEVELS = 5
SHUNT = 0.01
RELAX = 0.8
LANES = 128

HALO = {1: 4, 2: 5, 3: 5, 4: 5}
WIDTH = {1: 24, 2: 24, 3: 16, 4: 16}
OFFSET = {1: 4, 2: 8, 3: 6, 4: 6}
PACK_E = {1: 0, 2: 32, 3: 48, 4: 56}
PACK_N = {1: 16, 2: 40, 3: 52, 4: 58}
PACK_ROWS = 64
MARGIN = 8
REACH = 3


def dot(a, b, dims=((1,), (0,))):
    return lax.dot_general(a, b, (dims, ((), ())), precision=HI, preferred_element_type=F32)


def iota(shape, dim):
    return lax.broadcasted_iota(jnp.int32, shape, dim)


def rows_loop(lo, hi, fn, unroll=1):
    def step(i, carry):
        fn(i)
        return carry

    lax.fori_loop(lo, hi, step, 0, unroll=unroll)


def source_kernel(block_rows, hit_ref, load_ref, rows_ref, cols_ref, cur_ref, out_ref):
    out_ref[...] = -load_ref[...]
    base = pl.program_id(0) * block_rows
    width = load_ref.shape[1]
    col_ids = iota((width, LANES), 0)

    def one(r, carry):
        @pl.when(hit_ref[base + r] > 0)
        def _():
            here = jnp.where(rows_ref[...] == base + r, cur_ref[...], 0.0)
            total = jnp.zeros((width, LANES), F32)
            for k in range(rows_ref.shape[0]):
                total += jnp.where(cols_ref[k : k + 1] == col_ids, here[k : k + 1], 0.0)
            out_ref[r] = out_ref[r] + total

        return carry

    lax.fori_loop(0, block_rows, one, 0)


def around(dist):
    return [
        (di, dd)
        for di in (-1, 0, 1)
        for dd in range(-dist, dist + 1)
        if (di, dd) != (0, 0)
    ]


def overlap(step, size, halo):
    low = max(0, step * size - halo)
    high = min(size, step * size + size + halo)
    return low, high - low


def cycle_kernel(
    n_grp, n_dev, n_rows, n_cols,
    src_hbm, east_ref, north_ref, tab_ref,
    out_hbm,
    s0, u0, v0, e0, n0, w0, nt_ext, pack,
    s1, s2, s3, s4, u1, u2, u3, u4, v1, v2, v3, v4,
    e1, e2, e3, e4, n1, n2, n3, n4, w1, w2, w3, w4,
    cx1, cx2, cx3, cx4,
    g_cond, g_src, x_ext, c5,
    m1, m2, m3, m4, m5, y1, y2, y3, y4, y5, t1, t2, t3, t4, t5, p1, p2, p3, p4, p5, p6,
    send, recv, local,
):
    g = lax.axis_index("grp")
    d = lax.axis_index("dev")
    S = {1: s1, 2: s2, 3: s3, 4: s4}
    U = {0: u0, 1: u1, 2: u2, 3: u3, 4: u4}
    V = {0: v0, 1: v1, 2: v2, 3: v3, 4: v4}
    E = {0: e0, 1: e1, 2: e2, 3: e3, 4: e4}
    N = {0: n0, 1: n1, 2: n2, 3: n3, 4: n4}
    W = {0: w0, 1: w1, 2: w2, 3: w3, 4: w4}
    CX = {1: cx1, 2: cx2, 3: cx3, 4: cx4}
    S[0] = s0
    MT = {1: m1, 2: m2, 3: m3, 4: m4, 5: m5}
    YY = {1: y1, 2: y2, 3: y3, 4: y4, 5: y5}
    YT = {1: t1, 2: t2, 3: t3, 4: t4, 5: t5}
    PP = {1: p1, 2: p2, 3: p3, 4: p4, 5: p5, 6: p6}
    R = {h: n_rows >> h for h in range(6)}
    C = {h: n_cols >> h for h in range(6)}
    H = dict(HALO)
    H[0] = 0
    JP = dict(WIDTH)
    JP[0] = n_cols
    OJ = dict(OFFSET)
    OJ[0] = 0

    counter = [0]

    def take():
        counter[0] += 1
        return counter[0] - 1

    def at(di, dd):
        return (lax.rem(g + (di + n_grp), n_grp), lax.rem(d + (dd + n_dev), n_dev))

    def remote(src, dst, device):
        m = take()
        return pltpu.make_async_remote_copy(
            src_ref=src, dst_ref=dst, send_sem=send.at[m], recv_sem=recv.at[m],
            device_id=device, device_id_type=MESH,
        )

    zd = lax.rem(d, 8)
    yd = d // 8
    near = [(o, (g, yd * 8 + lax.rem(zd + o, 8))) for o in range(1, 8)]
    far = [
        (lax.rem(g + a, n_grp), lax.rem(yd + b, 4) * 8 + zd)
        for a in range(n_grp)
        for b in range(4)
        if (a, b) != (0, 0)
    ]
    partners = [at(di, dd) for di, dd in around(REACH)] + [dev for _, dev in near] + far

    barrier = pltpu.get_barrier_semaphore()
    for dev in partners:
        pl.semaphore_signal(barrier, inc=1, device_id=dev, device_id_type=MESH)

    own_rows = pl.ds(0, n_rows)
    fetch = pltpu.make_async_copy(src_hbm, s0, local.at[0])
    fetch.start()

    def conductance(cls):
        value = jnp.full(cls.shape, tab_ref[0], F32)
        for c in range(1, 8):
            value = jnp.where(cls == c, tab_ref[c], value)
        return value

    rows_c = iota((n_rows, n_cols), 0)
    cols_c = iota((n_rows, n_cols), 1)
    east = conductance(east_ref[...])
    east = jnp.where((rows_c == n_rows - 1) & (g == n_grp - 1), 0.0, east)
    north = conductance(north_ref[...])
    north = jnp.where((cols_c == n_cols - 1) & (d == n_dev - 1), 0.0, north)
    et = east.T
    nt = north.T
    nt_ext[pl.ds(MARGIN, n_cols), :] = nt

    packed = jnp.zeros((PACK_ROWS, LANES), F32)
    ri = iota((n_rows, LANES), 0)
    li = iota((n_rows, LANES), 1)
    pr = iota((PACK_ROWS, n_cols), 0)
    pj = iota((PACK_ROWS, n_cols), 1)
    for h in range(1, LEVELS):
        f = 1 << h
        last = jnp.where(ri == li * f + (f - 1), 1.0, 0.0)
        every = jnp.where(ri // f == li, 1.0, 0.0)
        qe = dot(et, last)
        qn = dot(nt, every)
        re, rn = pr - PACK_E[h], pr - PACK_N[h]
        pick_e = jnp.where((re >= 0) & (re < C[h]) & (pj // f == re), 1.0, 0.0)
        pick_n = jnp.where((rn >= 0) & (rn < C[h]) & (pj == rn * f + (f - 1)), 1.0, 0.0)
        packed += dot(pick_e, qe) + dot(pick_n, qn)
    pack[1, REACH] = packed

    si = iota((R[5], n_rows), 0)
    ci = iota((R[5], n_rows), 1)
    fe = jnp.where(ci == si * 32 + 31, 1.0, 0.0)
    fn_ = jnp.where(ci // 32 == si, 1.0, 0.0)
    e5 = jnp.sum(dot(fe, east), axis=1, keepdims=True)
    n5s = dot(fn_, north)
    n5 = jnp.sum(jnp.where(iota(n5s.shape, 1) == n_cols - 1, n5s, 0.0), axis=1, keepdims=True)
    both = jnp.where(iota((R[5], LANES), 1) < 64, e5, n5)
    mine8 = pl.ds(pl.multiple_of(g * 8, 8), 8)
    g_cond[d, mine8, :] = both

    pl.semaphore_wait(barrier, len(partners))

    def gather_near(buf):
        return [
            remote(buf.at[d, mine8, :], buf.at[d, mine8, :], dev) for _, dev in near
        ]

    def gather_far(buf):
        slab = pl.ds(pl.multiple_of(yd * 8, 8), 8)
        return [remote(buf.at[slab, mine8, :], buf.at[slab, mine8, :], dev) for dev in far]

    def start(copies):
        for c in copies:
            c.start()

    def wait(copies):
        for c in copies:
            c.wait()

    north_edge = [
        remote(nt_ext.at[pl.ds(MARGIN + n_cols - 1, 1), :], nt_ext.at[pl.ds(MARGIN - 1, 1), :], at(0, 1))
    ]
    start(north_edge)
    cond_near = gather_near(g_cond)
    start(cond_near)
    pack_copies = []
    for di, dd in around(REACH):
        lo = {0: 0, 1: 0, 2: 48, 3: 56}[abs(dd)]
        part = pl.ds(lo, PACK_ROWS - lo)
        pack_copies.append(
            remote(pack.at[1, REACH, part, :], pack.at[1 - di, REACH - dd, part, :], at(di, dd))
        )
    start(pack_copies)

    def spread(block, lane, width):
        ids = iota(block.shape, 1)
        col = jnp.sum(jnp.where(ids == lane, block, 0.0), axis=1, keepdims=True)
        return jnp.broadcast_to(col, (width, LANES))

    for half in range(n_rows // LANES):
        blk = et[:, half * LANES : (half + 1) * LANES]

        def fill(i, blk=blk, half=half):
            e0[half * LANES + i + 1] = spread(blk, i, n_cols)

        rows_loop(0, LANES, fill, unroll=4)
    east_edge = [remote(e0.at[n_rows], e0.at[0], at(1, 0))]
    start(east_edge)
    wait(north_edge)
    for half in range(n_rows // LANES):
        blk = nt_ext[:, half * LANES : (half + 1) * LANES]

        def fill(i, blk=blk, half=half):
            n0[half * LANES + i + 1] = spread(blk, i, n_cols + MARGIN)

        rows_loop(0, LANES, fill, unroll=4)

    wait(cond_near)
    cond_far = gather_far(g_cond)
    start(cond_far)
    wait(east_edge)

    def win(h, shift=0):
        return pl.ds(MARGIN + shift, JP[h])

    def diagonal(h, r, shunt):
        return shunt + E[h][r] + E[h][r - 1] + N[h][r, win(h), :] + N[h][r, win(h, -1), :]

    def around_sum(h, ref, r):
        return (
            E[h][r] * ref[r + 1, win(h), :]
            + E[h][r - 1] * ref[r - 1, win(h), :]
            + N[h][r, win(h), :] * ref[r, win(h, 1), :]
            + N[h][r, win(h, -1), :] * ref[r, win(h, -1), :]
        )

    def set_weights(h):
        shunt = SHUNT * 4.0**h

        def fill(r):
            W[h][r] = RELAX / diagonal(h, r, shunt)

        rows_loop(1, R[h] + 2 * H[h] + 1, fill, unroll=2)

    def s_row(h, r):
        return s0[r - 1] if h == 0 else S[h][r]

    def first(h):
        def fill(r):
            U[h][r, win(h), :] = W[h][r] * s_row(h, r)

        rows_loop(1, R[h] + 2 * H[h] + 1, fill, unroll=2)

    def presmooth(h):
        lo = 1 if h == 0 else 2

        def fill(r):
            V[h][r, win(h), :] = W[h][r] * (1.2 * s_row(h, r) + around_sum(h, U[h], r))

        rows_loop(lo, R[h] + 2 * H[h] + 2 - lo, fill, unroll=2)

    def restrict(h):
        shunt = SHUNT * 4.0**h

        def residual(r):
            return (
                s_row(h, r)
                + around_sum(h, V[h], r)
                - diagonal(h, r, shunt) * V[h][r, win(h), :]
            )

        base = H[h] + 1

        def fill(q):
            U[h][q, win(h), :] = residual(base + 2 * q) + residual(base + 2 * q + 1)

        rows_loop(0, R[h + 1], fill, unroll=2)
        cc = C[h + 1]

        def halve(q):
            a = U[h][q, pl.ds(MARGIN + OJ[h], cc, stride=2), :]
            b = U[h][q, pl.ds(MARGIN + OJ[h] + 1, cc, stride=2), :]
            if h == LEVELS - 1:
                g_src[d, pl.ds(g * 8 + q, 1), :] = a + b
            else:
                S[h + 1][q + H[h + 1] + 1, pl.ds(OJ[h + 1], cc), :] = a + b

        rows_loop(0, R[h + 1], halve, unroll=2)

    def edges(ref):
        rows = pl.ds(1, n_rows)
        cols = pl.ds(MARGIN, n_cols)
        return [
            remote(ref.at[rows, pl.ds(MARGIN + n_cols - 1, 1), :], ref.at[rows, pl.ds(MARGIN - 1, 1), :], at(0, 1)),
            remote(ref.at[rows, pl.ds(MARGIN, 1), :], ref.at[rows, pl.ds(MARGIN + n_cols, 1), :], at(0, -1)),
            remote(ref.at[n_rows, cols, :], ref.at[0, cols, :], at(1, 0)),
            remote(ref.at[1, cols, :], ref.at[n_rows + 1, cols, :], at(-1, 0)),
        ]

    def halos(h):
        dist = -(-H[h] // C[h])
        copies = []
        for di, dd in around(dist):
            i0, ni = overlap(di, R[h], H[h])
            j0, nj = overlap(dd, C[h], H[h])
            src = S[h].at[pl.ds(i0 + H[h] + 1, ni), pl.ds(j0 + OJ[h], nj), :]
            dst = S[h].at[
                pl.ds(i0 - di * R[h] + H[h] + 1, ni), pl.ds(j0 - dd * C[h] + OJ[h], nj), :
            ]
            copies.append(remote(src, dst, at(di, dd)))
        return copies

    set_weights(0)
    fetch.wait()
    first(0)
    u_edges = edges(u0)
    start(u_edges)

    wait(pack_copies)
    for h in range(1, LEVELS):
        width = MARGIN + JP[h]
        for t, base in ((0, PACK_E[h]), (1, PACK_N[h])):
            for di in range(3):
                for dd in range(-REACH, REACH + 1):
                    first_j = dd * C[h] + OJ[h] + MARGIN
                    lo = max(first_j, MARGIN - 1)
                    hi = min(first_j + C[h], width)
                    if hi > lo and abs(dd) <= -(-(H[h] + 1) // C[h]):
                        CX[h][t, di, pl.ds(lo, hi - lo), :] = pack[
                            di, dd + REACH, pl.ds(base + lo - first_j, hi - lo), :
                        ]

        def fill(i, di, shift, h=h, width=width):
            r = i + H[h] + 1 + shift
            E[h][r] = spread(CX[h][0, di, pl.ds(MARGIN, JP[h]), :], i, JP[h])
            N[h][r] = spread(CX[h][1, di], i, width)

        rows_loop(R[h] - H[h] - 1, R[h], functools.partial(fill, di=0, shift=-R[h]))
        rows_loop(0, R[h], functools.partial(fill, di=1, shift=0), unroll=4)
        rows_loop(0, H[h] + 1, functools.partial(fill, di=2, shift=R[h]))
        set_weights(h)

    wait(cond_far)

    nb = n_dev
    nn = n_grp * R[5]
    sub = iota((nn, nn), 0)
    lane = iota((nn, nn), 1)
    eye = sub == lane
    shunt5 = SHUNT * 4.0**LEVELS

    def coarse_block(k):
        both = g_cond[k]
        ee = both[:, :nn]
        low = pltpu.roll(both, 1, 0)[:, :nn]
        nc = pltpu.roll(both, 64, 1)[:, :nn]
        before = pltpu.roll(g_cond[(k - 1) % nb], 64, 1)[:, :nn]
        block = jnp.where(eye, shunt5 + ee + low + nc + before, 0.0)
        block = jnp.where(lane == sub + 1, -ee, block)
        block = jnp.where(lane == sub - 1, -low, block)
        return block, jnp.where(eye, -nc, 0.0), jnp.where(eye, -before, 0.0)

    def invert(ref):
        count = ref.shape[0]
        l3 = iota((count, nn, nn), 2)
        s3_ = iota((count, nn, nn), 1)
        lr = iota((count, 1, nn), 2)

        def step(k, carry):
            mat = ref[...]
            row = ref[:, pl.ds(k, 1), :]
            pivot = 1.0 / jnp.sum(jnp.where(lr == k, row, 0.0), axis=2, keepdims=True)
            col = jnp.sum(jnp.where(l3 == k, mat, 0.0), axis=2, keepdims=True)
            col = jnp.where(s3_ == k, -1.0, col)
            row = jnp.where(lr == k, pivot, row * pivot)
            ref[...] = jnp.where((l3 == k) | (s3_ == k), 0.0, mat) - col * row
            return carry

        lax.fori_loop(0, nn, step, 0)

    even = []
    for q in range(nb // 2):
        even.append(coarse_block(2 * q)[0])
        block, right, left = coarse_block(2 * q + 1)
        PP[1][q] = block
        MT[1][q] = jnp.concatenate([right, left], axis=0)
    for lev in range(1, 6):
        half = nb >> lev
        invert(PP[lev])
        zs = []
        for q in range(half):
            mt = MT[lev][q]
            inv = PP[lev][q]
            yt = dot(mt, inv)
            YT[lev][q] = yt
            YY[lev][q] = dot(inv, mt, ((1,), (1,)))
            zs.append(dot(yt, mt, ((1,), (1,))))
        new = []
        for q in range(half):
            block = even[q] - zs[q][nn:, nn:]
            if q > 0:
                block = block - zs[q - 1][:nn, :nn]
            new.append(block)
        if lev == 5:
            PP[6][0] = new[0]
        else:
            for q in range(half // 2):
                odd = 2 * q + 1
                PP[lev + 1][q] = new[odd]
                MT[lev + 1][q] = jnp.concatenate(
                    [-zs[odd][:nn, nn:], -zs[odd - 1][nn:, :nn]], axis=0
                )
            even = new[0::2]
    invert(PP[6])

    wait(u_edges)
    presmooth(0)
    v_edges = edges(v0)
    start(v_edges)
    wait(v_edges)
    restrict(0)
    for h in range(1, LEVELS):
        copies = halos(h)
        start(copies)
        wait(copies)
        first(h)
        presmooth(h)
        restrict(h)
    src_near = gather_near(g_src)
    start(src_near)
    wait(src_near)
    src_far = gather_far(g_src)
    start(src_far)
    x_ext[...] = jnp.zeros_like(x_ext)
    wait(src_far)

    for lev in range(1, 6):
        st = 1 << (lev - 1)
        for q in range(nb >> lev):
            odd = (2 * q + 1) * st
            upd = dot(YT[lev][q], g_src[odd])
            g_src[odd - st] = g_src[odd - st] - upd[nn:]
            if odd + st < nb:
                g_src[odd + st] = g_src[odd + st] - upd[:nn]
    inner = pl.ds(MARGIN, nn)
    x_ext[4, inner, :] = dot(PP[6][0], g_src[0])
    for lev in range(5, 0, -1):
        st = 1 << (lev - 1)
        for q in range(nb >> lev):
            odd = (2 * q + 1) * st
            x = dot(PP[lev][q], g_src[odd])
            y = YY[lev][q]
            x = x - dot(y[:, nn:], x_ext[4 + odd - st, inner, :])
            if odd + st < nb:
                x = x - dot(y[:, :nn], x_ext[4 + odd + st, inner, :])
            x_ext[4 + odd, inner, :] = x

    for k in range(8):
        part = x_ext[d + 1 + k, pl.ds(pl.multiple_of(g * 8, 8), 24), :]
        for i in range(12):
            c5[i, k : k + 1, :] = part[6 + i : 7 + i]

    def smooth(h, dst, ref, halo):
        lo = H[h] + 1 - halo if h else 1
        hi = R[h] + H[h] + 1 + halo if h else n_rows + 1

        def fill(r):
            dst[r, win(h), :] = 0.2 * ref[r, win(h), :] + W[h][r] * (
                s_row(h, r) + around_sum(h, ref, r)
            )

        rows_loop(lo, hi, fill, unroll=2)

    for h in range(LEVELS - 1, 0, -1):
        p = H[h] - 1
        first_q = -(-p // 2)
        size = JP[h] // 2

        def lift(q, h=h, size=size):
            if h == LEVELS - 1:
                coarse = c5[q + 2]
            else:
                cofs = MARGIN + OJ[h + 1] - OJ[h] // 2
                coarse = V[h + 1][q + H[h + 1] + 1, pl.ds(cofs, size), :]
            for a in range(2):
                r = 2 * q + a + H[h] + 1
                for b in range(2):
                    cols = pl.ds(MARGIN + b, size, stride=2)
                    V[h][r, cols, :] = V[h][r, cols, :] + coarse

        rows_loop(-first_q, R[h] // 2 + first_q, lift, unroll=2)
        smooth(h, U[h], V[h], p - 1)
        smooth(h, V[h], U[h], p - 2)

    half_cols = n_cols // 2

    def lift0(q, rows):
        coarse = V[1][q + H[1] + 1, pl.ds(MARGIN + OJ[1] - 1, half_cols + 2), :]
        for a in rows:
            r = 2 * q + a + 1
            for b in range(2):
                cols = pl.ds(MARGIN - 2 + b, half_cols + 2, stride=2)
                v0[r, cols, :] = v0[r, cols, :] + coarse

    lift0(-1, (1,))
    rows_loop(0, n_rows // 2, functools.partial(lift0, rows=(0, 1)), unroll=2)
    lift0(n_rows // 2, (0,))
    smooth(0, u0, v0, 0)
    m_edges = edges(u0)
    start(m_edges)
    wait(m_edges)

    def last(r):
        s0[r - 1] = 0.2 * u0[r, win(0), :] + W[0][r] * (s0[r - 1] + around_sum(0, u0, r))

    rows_loop(1, n_rows + 1, last, unroll=2)
    done = pltpu.make_async_copy(s0, out_hbm, local.at[0])
    done.start()
    done.wait()
    assert counter[0] <= N_COPIES, counter[0]


N_COPIES = 150


def body(n_grp, n_dev, load, east_class, north_class, cond_table, taps, tap_current):
    n_rows, n_cols, cands = load.shape
    row0 = lax.axis_index("grp") * n_rows
    col0 = lax.axis_index("dev") * n_cols
    rows = (taps // (n_dev * n_cols) - row0).T
    cols = (taps % (n_dev * n_cols) - col0).T
    inside = (cols >= 0) & (cols < n_cols)
    marked = jnp.where(inside, rows, -1).reshape(-1)
    hit = jnp.any(
        marked[None, :] == jnp.arange(n_rows, dtype=jnp.int32)[:, None], axis=1
    ).astype(jnp.int32)
    blk = 32
    whole = lambda shape: pl.BlockSpec(shape, lambda i, *_: (0,) * len(shape))
    source = pl.pallas_call(
        functools.partial(source_kernel, blk),
        grid_spec=pltpu.PrefetchScalarGridSpec(
            num_scalar_prefetch=1,
            grid=(n_rows // blk,),
            in_specs=[
                pl.BlockSpec((blk, n_cols, cands), lambda i, *_: (i, 0, 0)),
                whole(rows.shape),
                whole(rows.shape),
                whole(rows.shape),
            ],
            out_specs=pl.BlockSpec((blk, n_cols, cands), lambda i, *_: (i, 0, 0)),
        ),
        out_shape=jax.ShapeDtypeStruct(load.shape, F32),
        compiler_params=pltpu.CompilerParams(vmem_limit_bytes=16 << 20),
    )(hit, load, rows, cols, tap_current.T)

    def vm(*shape):
        return pltpu.VMEM(shape, F32)

    ext0 = (n_rows + 2, n_cols + 2 * MARGIN, LANES)
    tall = {h: (n_rows >> h) + 2 * HALO[h] + 2 for h in range(1, LEVELS)}
    levels = range(1, LEVELS)
    nn = n_dev
    scratch = [
        vm(n_rows, n_cols, LANES), vm(*ext0), vm(*ext0),
        vm(n_rows + 1, n_cols, LANES), vm(n_rows + 1, n_cols + MARGIN, LANES),
        vm(n_rows + 1, n_cols, LANES), vm(n_cols + MARGIN, n_rows),
        vm(3, 2 * REACH + 1, PACK_ROWS, LANES),
    ]
    scratch += [vm(tall[h], WIDTH[h], LANES) for h in levels]
    scratch += [vm(tall[h], WIDTH[h] + 2 * MARGIN, LANES) for h in levels] * 2
    scratch += [vm(tall[h], WIDTH[h], LANES) for h in levels]
    scratch += [vm(tall[h], WIDTH[h] + MARGIN, LANES) for h in levels]
    scratch += [vm(tall[h], WIDTH[h], LANES) for h in levels]
    scratch += [vm(2, 3, WIDTH[h] + MARGIN, LANES) for h in levels]
    scratch += [vm(n_dev, 32, LANES), vm(n_dev, 32, LANES), vm(n_dev + 8, 32 + 16, LANES), vm(12, 8, LANES)]
    scratch += [vm(nn >> l, 64, 32) for l in range(1, 6)]
    scratch += [vm(nn >> l, 32, 64) for l in range(1, 6)]
    scratch += [vm(nn >> l, 64, 32) for l in range(1, 6)]
    scratch += [vm(nn >> l, 32, 32) for l in range(1, 6)] + [vm(1, 32, 32)]
    scratch += [
        pltpu.SemaphoreType.DMA((N_COPIES,)),
        pltpu.SemaphoreType.DMA((N_COPIES,)),
        pltpu.SemaphoreType.DMA((1,)),
    ]
    return pl.pallas_call(
        functools.partial(cycle_kernel, n_grp, n_dev, n_rows, n_cols),
        out_shape=jax.ShapeDtypeStruct(load.shape, F32),
        in_specs=[
            pl.BlockSpec(memory_space=pl.ANY),
            pl.BlockSpec(memory_space=pltpu.VMEM),
            pl.BlockSpec(memory_space=pltpu.VMEM),
            pl.BlockSpec(memory_space=pltpu.SMEM),
        ],
        out_specs=pl.BlockSpec(memory_space=pl.ANY),
        scratch_shapes=scratch,
        compiler_params=pltpu.CompilerParams(
            collective_id=0, has_side_effects=True, vmem_limit_bytes=63 << 20
        ),
    )(source, east_class, north_class, cond_table)


def solution(mesh):
    return jax.shard_map(
        functools.partial(body, mesh.shape["grp"], mesh.shape["dev"]),
        mesh=mesh,
        in_specs=(P("grp", "dev", None), P("grp", "dev"), P("grp", "dev"), P(), P(), P()),
        out_specs=P("grp", "dev", None),
        check_vma=False,
    )
```

time: 939 us -> 167 us (0.18)
  the two profiles are of different devices: /device:TPU:8 before, /device:TPU:1 now
where the time goes in v1:
time: 167 us
  Pallas kernels  153 us (92%)
  local copies, waits for them, and re-layouts  12.5 us (7%)
    pallas_call x1, Pallas kernels, body(): pl.pallas_call(functools.partial(cycle_kernel, n_grp, n_dev, n_rows, n_co...  148 us
    unnamed x9, local copies, waits for them, and re-layouts  12.5 us
    pallas_call x1, Pallas kernels, body(): pl.pallas_call(functools.partial(source_kernel, blk), grid_spec=pltpu.Pre...  5 us

profile of v1, /device:TPU:1, one launch (start us, length us, event | category | flops | bytes accessed | tf_op | source)
XLA Modules:
  0.0 166.5 jit_solution(10161142892183267705)
XLA Ops:
  0.0 0.7 select_bitcast_fusion
  0.7 0.3 fusion
  1.1 1.5 copy.9.east_ref
  2.6 1.5 copy.10.north_ref
  4.1 0.0 copy-start.1
  4.1 2.2 %copy-done.1 = f32[256,32,128]{2,1,0:T(8,128)S(1)} copy-done((f32[256,32,128]{2,1,0:T(8,128)S(1)}, f32[256,32,128]{2,1,0:T(8,128)}, u32[]{:S(2)}) %copy-start.1) | copy-done | bytes 4194328
  6.2 0.0 copy-start.2
  6.2 0.7 copy-done.2
  6.9 5.0 %shard_map.64.src_hbm = f32[256,32,128]{2,1,0:T(8,128)S(1)} custom-call(s32[256]{0:T(256)S(1)} %convert_element_type.3.hit_ref, f32[256,32,128]{2,1,0:T(8,128)S(1)} %copy-done.1, s32[16,128]{1,0:T(8,128)S(1)} %get-tuple-element.7.rows_ref, s32[16,128]{1,0:T(8,128)S(1)} %get-tuple-element.6.cols_ref, f32[16,128]{1,0:T(8,128)S(1)} %bitcast.9), custom_call_target="tpu_custom_call" | custom-call | tf_op jit(solution)/shard_map/pallas_call | solution.py:571
  12.0 0.0 copy-start
  12.0 2.0 %copy-done = f32[256,32,128]{2,1,0:T(8,128)} copy-done((f32[256,32,128]{2,1,0:T(8,128)}, f32[256,32,128]{2,1,0:T(8,128)S(1)}, u32[]{:S(2)}) %copy-start) | copy-done | bytes 4194328
  14.0 147.9 %shard_map.65 = f32[256,32,128]{2,1,0:T(8,128)} custom-call(f32[256,32,128]{2,1,0:T(8,128)} %copy-done, s32[256,32]{1,0:T(8,128)} %copy.9.east_ref, s32[256,32]{1,0:T(8,128)} %copy.10.north_ref, f32[8]{0:T(128)} %tab_ref.1), custom_call_target="tpu_custom_call" | custom-call | tf_op jit(solution)/shard_map/pallas_call | solution.py:617
  161.9 4.6 %copy.12 = f32[256,32,128]{2,1,0:T(8,128)} copy(f32[256,32,128]{2,1,0:T(8,128)} %shard_map.65) | data formatting | bytes 8388608
  (1 shorter events, 0.0 us)
Async XLA Ops:
  4.1 2.2 %copy-start.1 = (f32[256,32,128]{2,1,0:T(8,128)S(1)}, f32[256,32,128]{2,1,0:T(8,128)}, u32[]{:S(2)}) copy-start(f32[256,32,128]{2,1,0:T(8,128)} %load_ref.1) | copy-start | bytes 12582916
  6.2 0.7 copy-start.2
  12.0 2.0 %copy-start = (f32[256,32,128]{2,1,0:T(8,128)}, f32[256,32,128]{2,1,0:T(8,128)S(1)}, u32[]{:S(2)}) copy-start(f32[256,32,128]{2,1,0:T(8,128)S(1)} %shard_map.64.src_hbm) | copy-start | bytes 12582916

commit v2 on v1

--- a/solution.py
+++ b/solution.py
@@ -23,6 +23,7 @@
 PACK_ROWS = 64
 MARGIN = 8
 REACH = 3
+TABLE_PART = 32
 
 
 def dot(a, b, dims=((1,), (0,))):
@@ -41,24 +42,54 @@
     lax.fori_loop(lo, hi, step, 0, unroll=unroll)
 
 
-def source_kernel(block_rows, hit_ref, load_ref, rows_ref, cols_ref, cur_ref, out_ref):
-    out_ref[...] = -load_ref[...]
-    base = pl.program_id(0) * block_rows
-    width = load_ref.shape[1]
-    col_ids = iota((width, LANES), 0)
-
-    def one(r, carry):
-        @pl.when(hit_ref[base + r] > 0)
+def tap_kernel(n_rows, n_cols, shift, taps_ref, cur_ref, table_hbm, slot_ref, table, sems):
+    far = 1 << 24
+    taps = taps_ref[...]
+    cur = cur_ref[...]
+    rows = jnp.right_shift(taps, shift) - lax.axis_index("grp") * n_rows
+    cols = jnp.bitwise_and(taps, (1 << shift) - 1) - lax.axis_index("dev") * n_cols
+    inside = (rows >= 0) & (rows < n_rows) & (cols >= 0) & (cols < n_cols)
+    rows = jnp.where(inside, rows, far)
+    col_ids = iota((n_cols, LANES), 0)
+
+    def clear(i, carry):
+        slot_ref[i] = 0
+        return carry
+
+    lax.fori_loop(0, n_rows, clear, 0, unroll=8)
+    table[0] = jnp.zeros((n_cols, LANES), F32)
+
+    def more(carry):
+        return carry[1] < far
+
+    def one(carry):
+        used, row = carry
+        following = jnp.min(jnp.where(rows > row, rows, far))
+        here = jnp.where(rows == row, cur, 0.0)
+        total = jnp.zeros((n_cols, LANES), F32)
+        for k in range(taps.shape[0]):
+            total += jnp.where(cols[k : k + 1] == col_ids, here[k : k + 1], 0.0)
+        table[used] = total
+        slot_ref[row] = used
+        return used + 1, following
+
+    used, _ = lax.while_loop(more, one, (jnp.int32(1), jnp.min(rows)))
+
+    def part(c):
+        at = pl.ds(c * TABLE_PART, TABLE_PART)
+        return pltpu.make_async_copy(table.at[at], table_hbm.at[at], sems.at[c])
+
+    for c in range(table.shape[0] // TABLE_PART):
+
+        @pl.when(used > c * TABLE_PART)
         def _():
-            here = jnp.where(rows_ref[...] == base + r, cur_ref[...], 0.0)
-            total = jnp.zeros((width, LANES), F32)
-            for k in range(rows_ref.shape[0]):
-                total += jnp.where(cols_ref[k : k + 1] == col_ids, here[k : k + 1], 0.0)
-            out_ref[r] = out_ref[r] + total
-
-        return carry
-
-    lax.fori_loop(0, block_rows, one, 0)
+            part(c).start()
+
+    for c in range(table.shape[0] // TABLE_PART):
+
+        @pl.when(used > c * TABLE_PART)
+        def _():
+            part(c).wait()
 
 
 def around(dist):
@@ -78,7 +109,7 @@
 
 def cycle_kernel(
     n_grp, n_dev, n_rows, n_cols,
-    src_hbm, east_ref, north_ref, tab_ref,
+    load_hbm, table_hbm, slot_ref, east_ref, north_ref, tab_ref,
     out_hbm,
     s0, u0, v0, e0, n0, w0, nt_ext, pack,
     s1, s2, s3, s4, u1, u2, u3, u4, v1, v2, v3, v4,
@@ -143,8 +174,14 @@
         pl.semaphore_signal(barrier, inc=1, device_id=dev, device_id_type=MESH)
 
     own_rows = pl.ds(0, n_rows)
-    fetch = pltpu.make_async_copy(src_hbm, s0, local.at[0])
+    fetch = pltpu.make_async_copy(load_hbm, s0, local.at[0])
     fetch.start()
+    fetch_table = pltpu.make_async_copy(
+        table_hbm.at[pl.ds(0, n_rows + 1)],
+        v0.at[pl.ds(0, n_rows + 1), pl.ds(MARGIN, n_cols), :],
+        local.at[1],
+    )
+    fetch_table.start()
 
     def conductance(cls):
         value = jnp.full(cls.shape, tab_ref[0], F32)
@@ -152,14 +189,12 @@
             value = jnp.where(cls == c, tab_ref[c], value)
         return value
 
-    rows_c = iota((n_rows, n_cols), 0)
-    cols_c = iota((n_rows, n_cols), 1)
-    east = conductance(east_ref[...])
-    east = jnp.where((rows_c == n_rows - 1) & (g == n_grp - 1), 0.0, east)
-    north = conductance(north_ref[...])
-    north = jnp.where((cols_c == n_cols - 1) & (d == n_dev - 1), 0.0, north)
-    et = east.T
-    nt = north.T
+    rows_c = iota((n_cols, n_rows), 1)
+    cols_c = iota((n_cols, n_rows), 0)
+    et = conductance(east_ref[...])
+    et = jnp.where((rows_c == n_rows - 1) & (g == n_grp - 1), 0.0, et)
+    nt = conductance(north_ref[...])
+    nt = jnp.where((cols_c == n_cols - 1) & (d == n_dev - 1), 0.0, nt)
     nt_ext[pl.ds(MARGIN, n_cols), :] = nt
 
     packed = jnp.zeros((PACK_ROWS, LANES), F32)
@@ -183,8 +218,8 @@
     ci = iota((R[5], n_rows), 1)
     fe = jnp.where(ci == si * 32 + 31, 1.0, 0.0)
     fn_ = jnp.where(ci // 32 == si, 1.0, 0.0)
-    e5 = jnp.sum(dot(fe, east), axis=1, keepdims=True)
-    n5s = dot(fn_, north)
+    e5 = jnp.sum(dot(fe, et, ((1,), (1,))), axis=1, keepdims=True)
+    n5s = dot(fn_, nt, ((1,), (1,)))
     n5 = jnp.sum(jnp.where(iota(n5s.shape, 1) == n_cols - 1, n5s, 0.0), axis=1, keepdims=True)
     both = jnp.where(iota((R[5], LANES), 1) < 64, e5, n5)
     mine8 = pl.ds(pl.multiple_of(g * 8, 8), 8)
@@ -279,6 +314,8 @@
 
     def first(h):
         def fill(r):
+            if h == 0:
+                s0[r - 1] = v0[slot_ref[r - 1], win(0), :] - s0[r - 1]
             U[h][r, win(h), :] = W[h][r] * s_row(h, r)
 
         rows_loop(1, R[h] + 2 * H[h] + 1, fill, unroll=2)
@@ -344,12 +381,12 @@
 
     set_weights(0)
     fetch.wait()
+    fetch_table.wait()
     first(0)
     u_edges = edges(u0)
     start(u_edges)
 
-    wait(pack_copies)
-    for h in range(1, LEVELS):
+    def spread_level(h):
         width = MARGIN + JP[h]
         for t, base in ((0, PACK_E[h]), (1, PACK_N[h])):
             for di in range(3):
@@ -362,7 +399,7 @@
                             di, dd + REACH, pl.ds(base + lo - first_j, hi - lo), :
                         ]
 
-        def fill(i, di, shift, h=h, width=width):
+        def fill(i, di, shift):
             r = i + H[h] + 1 + shift
             E[h][r] = spread(CX[h][0, di, pl.ds(MARGIN, JP[h]), :], i, JP[h])
             N[h][r] = spread(CX[h][1, di], i, width)
@@ -371,8 +408,6 @@
         rows_loop(0, R[h], functools.partial(fill, di=1, shift=0), unroll=4)
         rows_loop(0, H[h] + 1, functools.partial(fill, di=2, shift=R[h]))
         set_weights(h)
-
-    wait(cond_far)
 
     nb = n_dev
     nn = n_grp * R[5]
@@ -410,13 +445,17 @@
 
         lax.fori_loop(0, nn, step, 0)
 
-    even = []
-    for q in range(nb // 2):
-        even.append(coarse_block(2 * q)[0])
-        block, right, left = coarse_block(2 * q + 1)
-        PP[1][q] = block
-        MT[1][q] = jnp.concatenate([right, left], axis=0)
-    for lev in range(1, 6):
+    even = {}
+
+    def matrices():
+        even[1] = []
+        for q in range(nb // 2):
+            even[1].append(coarse_block(2 * q)[0])
+            block, right, left = coarse_block(2 * q + 1)
+            PP[1][q] = block
+            MT[1][q] = jnp.concatenate([right, left], axis=0)
+
+    def eliminate(lev):
         half = nb >> lev
         invert(PP[lev])
         zs = []
@@ -429,7 +468,7 @@
             zs.append(dot(yt, mt, ((1,), (1,))))
         new = []
         for q in range(half):
-            block = even[q] - zs[q][nn:, nn:]
+            block = even[lev][q] - zs[q][nn:, nn:]
             if q > 0:
                 block = block - zs[q - 1][:nn, :nn]
             new.append(block)
@@ -442,27 +481,35 @@
                 MT[lev + 1][q] = jnp.concatenate(
                     [-zs[odd][:nn, nn:], -zs[odd - 1][nn:, :nn]], axis=0
                 )
-            even = new[0::2]
-    invert(PP[6])
-
+            even[lev + 1] = new[0::2]
+
+    wait(pack_copies)
+    spread_level(1)
     wait(u_edges)
     presmooth(0)
     v_edges = edges(v0)
     start(v_edges)
+    for h in range(2, LEVELS):
+        spread_level(h)
+    wait(cond_far)
+    matrices()
     wait(v_edges)
     restrict(0)
     for h in range(1, LEVELS):
         copies = halos(h)
         start(copies)
+        eliminate(h)
         wait(copies)
         first(h)
         presmooth(h)
         restrict(h)
     src_near = gather_near(g_src)
     start(src_near)
+    eliminate(5)
     wait(src_near)
     src_far = gather_far(g_src)
     start(src_far)
+    invert(PP[6])
     x_ext[...] = jnp.zeros_like(x_ext)
     wait(src_far)
 
@@ -537,53 +584,79 @@
     lift0(-1, (1,))
     rows_loop(0, n_rows // 2, functools.partial(lift0, rows=(0, 1)), unroll=2)
     lift0(n_rows // 2, (0,))
-    smooth(0, u0, v0, 0)
-    m_edges = edges(u0)
-    start(m_edges)
-    wait(m_edges)
-
-    def last(r):
-        s0[r - 1] = 0.2 * u0[r, win(0), :] + W[0][r] * (s0[r - 1] + around_sum(0, u0, r))
-
-    rows_loop(1, n_rows + 1, last, unroll=2)
-    done = pltpu.make_async_copy(s0, out_hbm, local.at[0])
-    done.start()
-    done.wait()
+    size = n_rows // PARTS
+    order = [PARTS - 1] + list(range(PARTS - 1))
+    flights = []
+    cols = pl.ds(MARGIN, n_cols)
+    for c in order:
+        lo = 1 + c * size
+
+        def fill(r):
+            u0[r, win(0), :] = 0.2 * v0[r, win(0), :] + W[0][r] * (
+                s0[r - 1] + around_sum(0, v0, r)
+            )
+
+        rows_loop(lo, lo + size, fill, unroll=2)
+        rows = pl.ds(lo, size)
+        mine = [
+            remote(u0.at[rows, pl.ds(MARGIN + n_cols - 1, 1), :], u0.at[rows, pl.ds(MARGIN - 1, 1), :], at(0, 1)),
+            remote(u0.at[rows, pl.ds(MARGIN, 1), :], u0.at[rows, pl.ds(MARGIN + n_cols, 1), :], at(0, -1)),
+        ]
+        if c == PARTS - 1:
+            last_row = remote(u0.at[n_rows, cols, :], u0.at[0, cols, :], at(1, 0))
+            mine.append(last_row)
+        if c == 0:
+            first_row = remote(u0.at[1, cols, :], u0.at[n_rows + 1, cols, :], at(-1, 0))
+            mine.append(first_row)
+        start(mine)
+        flights.append(mine[:2])
+    done = []
+    for c, mine in zip(order, flights):
+        wait(mine)
+        if c == PARTS - 1:
+            first_row.wait()
+        if c == 0:
+            last_row.wait()
+
+        def last(r):
+            s0[r - 1] = 0.2 * u0[r, win(0), :] + W[0][r] * (
+                s0[r - 1] + around_sum(0, u0, r)
+            )
+
+        rows_loop(1 + c * size, 1 + c * size + size, last, unroll=2)
+        rows = pl.ds(c * size, size)
+        done.append(pltpu.make_async_copy(s0.at[rows], out_hbm.at[rows], local.at[2 + c]))
+        done[-1].start()
+    wait(done)
     assert counter[0] <= N_COPIES, counter[0]
 
 
-N_COPIES = 150
+N_COPIES = 160
+PARTS = 4
 
 
 def body(n_grp, n_dev, load, east_class, north_class, cond_table, taps, tap_current):
     n_rows, n_cols, cands = load.shape
-    row0 = lax.axis_index("grp") * n_rows
-    col0 = lax.axis_index("dev") * n_cols
-    rows = (taps // (n_dev * n_cols) - row0).T
-    cols = (taps % (n_dev * n_cols) - col0).T
-    inside = (cols >= 0) & (cols < n_cols)
-    marked = jnp.where(inside, rows, -1).reshape(-1)
-    hit = jnp.any(
-        marked[None, :] == jnp.arange(n_rows, dtype=jnp.int32)[:, None], axis=1
-    ).astype(jnp.int32)
-    blk = 32
-    whole = lambda shape: pl.BlockSpec(shape, lambda i, *_: (0,) * len(shape))
-    source = pl.pallas_call(
-        functools.partial(source_kernel, blk),
-        grid_spec=pltpu.PrefetchScalarGridSpec(
-            num_scalar_prefetch=1,
-            grid=(n_rows // blk,),
-            in_specs=[
-                pl.BlockSpec((blk, n_cols, cands), lambda i, *_: (i, 0, 0)),
-                whole(rows.shape),
-                whole(rows.shape),
-                whole(rows.shape),
-            ],
-            out_specs=pl.BlockSpec((blk, n_cols, cands), lambda i, *_: (i, 0, 0)),
-        ),
-        out_shape=jax.ShapeDtypeStruct(load.shape, F32),
-        compiler_params=pltpu.CompilerParams(vmem_limit_bytes=16 << 20),
-    )(hit, load, rows, cols, tap_current.T)
+    slots = -(-(n_rows + 1) // TABLE_PART) * TABLE_PART
+    total = n_dev * n_cols
+    assert total & (total - 1) == 0
+    table, slot = pl.pallas_call(
+        functools.partial(tap_kernel, n_rows, n_cols, total.bit_length() - 1),
+        in_specs=[pl.BlockSpec(memory_space=pltpu.VMEM)] * 2,
+        out_specs=[
+            pl.BlockSpec(memory_space=pl.ANY),
+            pl.BlockSpec(memory_space=pltpu.SMEM),
+        ],
+        out_shape=[
+            jax.ShapeDtypeStruct((slots, n_cols, cands), F32),
+            jax.ShapeDtypeStruct((n_rows,), jnp.int32),
+        ],
+        scratch_shapes=[
+            pltpu.VMEM((slots, n_cols, cands), F32),
+            pltpu.SemaphoreType.DMA((slots // TABLE_PART,)),
+        ],
+        compiler_params=pltpu.CompilerParams(vmem_limit_bytes=60 << 20),
+    )(taps.T, tap_current.T)
 
     def vm(*shape):
         return pltpu.VMEM(shape, F32)
@@ -612,13 +685,15 @@
     scratch += [
         pltpu.SemaphoreType.DMA((N_COPIES,)),
         pltpu.SemaphoreType.DMA((N_COPIES,)),
-        pltpu.SemaphoreType.DMA((1,)),
+        pltpu.SemaphoreType.DMA((2 + PARTS,)),
     ]
     return pl.pallas_call(
         functools.partial(cycle_kernel, n_grp, n_dev, n_rows, n_cols),
         out_shape=jax.ShapeDtypeStruct(load.shape, F32),
         in_specs=[
             pl.BlockSpec(memory_space=pl.ANY),
+            pl.BlockSpec(memory_space=pl.ANY),
+            pl.BlockSpec(memory_space=pltpu.SMEM),
             pl.BlockSpec(memory_space=pltpu.VMEM),
             pl.BlockSpec(memory_space=pltpu.VMEM),
             pl.BlockSpec(memory_space=pltpu.SMEM),
@@ -628,7 +703,7 @@
         compiler_params=pltpu.CompilerParams(
             collective_id=0, has_side_effects=True, vmem_limit_bytes=63 << 20
         ),
-    )(source, east_class, north_class, cond_table)
+    )(load, table, slot, east_class.T, north_class.T, cond_table)
 
 
 def solution(mesh):

time: 167 us -> 125 us (0.75)
  Pallas kernels: 153 us -> 119 us
  local copies, waits for them, and re-layouts: 12.5 us -> 4.64 us
    pallas_call x1, Pallas kernels: 148 us -> 114 us  [body(): pl.pallas_call(functools.partial(cycle_kernel, n_grp, n_dev, n_rows, n_co...]
    unnamed x9 -> x1, local copies, waits for them, and re-layouts: 12.5 us -> 4.64 us
where the time goes in v2:
time: 125 us; the launch traced here: 124 us
  Pallas kernels  119 us (95%)
  local copies, waits for them, and re-layouts  4.64 us (4%)
    pallas_call x1, Pallas kernels, body(): pl.pallas_call(functools.partial(cycle_kernel, n_grp, n_dev, n_rows, n_co...  114 us
    pallas_call x1, Pallas kernels, body(): pl.pallas_call(functools.partial(tap_kernel, n_rows, n_cols, total.bit_le...  5.59 us
    unnamed x1, local copies, waits for them, and re-layouts  4.64 us

profile of v2, /device:TPU:1, one launch (start us, length us, event | category | flops | bytes accessed | tf_op | source)
XLA Modules:
  0.0 123.9 jit_solution(5958448419534378569)
XLA Ops:
  0.0 5.6 %shard_map.64 = (f32[288,32,128]{2,1,0:T(8,128)}, s32[256]{0:T(256)}) custom-call(s32[16,128]{1,0:T(8,128)} %bitcast.6, f32[16,128]{1,0:T(8,128)} %bitcast.7), custom_call_target="tpu_custom_call" | custom-call | tf_op jit(solution)/shard_map/pallas_call | solution.py:643
  5.6 113.6 %shard_map.65 = f32[256,32,128]{2,1,0:T(8,128)} custom-call(f32[256,32,128]{2,1,0:T(8,128)} %load_hbm.1, f32[288,32,128]{2,1,0:T(8,128)} %get-tuple-element.7.table_hbm, s32[256]{0:T(256)} %get-tuple-element.8.slot_ref, s32[32,256]{1,0:T(8,128)} %bitcast.4, s32[32,256]{1,0:T(8,128)} %bitcast.5, f32[8]{0:T(128)} %tab_ref.1), custom_call_target="tpu_custom_call" | custom-call | tf_op jit(solution)/shard_map/pallas_call | solution.py:690
  119.2 4.6 %copy.8 = f32[256,32,128]{2,1,0:T(8,128)} copy(f32[256,32,128]{2,1,0:T(8,128)} %shard_map.65) | data formatting | bytes 8388608

commit v3 on v2

--- a/solution.py
+++ b/solution.py
@@ -111,7 +111,7 @@
     n_grp, n_dev, n_rows, n_cols,
     load_hbm, table_hbm, slot_ref, east_ref, north_ref, tab_ref,
     out_hbm,
-    s0, u0, v0, e0, n0, w0, nt_ext, pack,
+    s0, u0, v0, e0, n0, w0, et_ref, nt_ext, pack,
     s1, s2, s3, s4, u1, u2, u3, u4, v1, v2, v3, v4,
     e1, e2, e3, e4, n1, n2, n3, n4, w1, w2, w3, w4,
     cx1, cx2, cx3, cx4,
@@ -260,27 +260,24 @@
     start(pack_copies)
 
     def spread(block, lane, width):
-        ids = iota(block.shape, 1)
-        col = jnp.sum(jnp.where(ids == lane, block, 0.0), axis=1, keepdims=True)
-        return jnp.broadcast_to(col, (width, LANES))
-
-    for half in range(n_rows // LANES):
-        blk = et[:, half * LANES : (half + 1) * LANES]
-
-        def fill(i, blk=blk, half=half):
-            e0[half * LANES + i + 1] = spread(blk, i, n_cols)
-
-        rows_loop(0, LANES, fill, unroll=4)
+        return jnp.broadcast_to(block[:, lane : lane + 1], (width, LANES))
+
+    et_ref[...] = et
+
+    def spread_part(dst, src, width):
+        def fill(half):
+            base = pl.multiple_of(half * LANES, LANES)
+            blk = src[:, pl.ds(base, LANES)]
+            for i in range(LANES):
+                dst[base + i + 1] = spread(blk, i, width)
+
+        rows_loop(0, n_rows // LANES, fill)
+
+    spread_part(e0, et_ref, n_cols)
     east_edge = [remote(e0.at[n_rows], e0.at[0], at(1, 0))]
     start(east_edge)
     wait(north_edge)
-    for half in range(n_rows // LANES):
-        blk = nt_ext[:, half * LANES : (half + 1) * LANES]
-
-        def fill(i, blk=blk, half=half):
-            n0[half * LANES + i + 1] = spread(blk, i, n_cols + MARGIN)
-
-        rows_loop(0, LANES, fill, unroll=4)
+    spread_part(n0, nt_ext, n_cols + MARGIN)
 
     wait(cond_near)
     cond_far = gather_far(g_cond)
@@ -293,13 +290,38 @@
     def diagonal(h, r, shunt):
         return shunt + E[h][r] + E[h][r - 1] + N[h][r, win(h), :] + N[h][r, win(h, -1), :]
 
-    def around_sum(h, ref, r):
-        return (
-            E[h][r] * ref[r + 1, win(h), :]
-            + E[h][r - 1] * ref[r - 1, win(h), :]
-            + N[h][r, win(h), :] * ref[r, win(h, 1), :]
-            + N[h][r, win(h, -1), :] * ref[r, win(h, -1), :]
-        )
+    def stencil(h, ref, lo, hi, emit, block=8):
+        def some(r0, count):
+            stencil_rows(h, ref, r0, count, emit)
+
+        full = (hi - lo) // block
+        rows_loop(0, full, lambda q: some(lo + q * block, block))
+        if lo + full * block < hi:
+            some(lo + full * block, hi - lo - full * block)
+
+    def stencil_rows(h, ref, r0, count, emit):
+        for t in range(JP[h] // 8):
+            here = pl.ds(8 * t, 8)
+            mid = pl.ds(MARGIN + 8 * t, 8)
+            up = pl.ds(MARGIN + 8 * t + 1, 8)
+            down = pl.ds(MARGIN + 8 * t - 1, 8)
+            below = ref[r0 - 1, mid, :]
+            centre = ref[r0, mid, :]
+            low = E[h][r0 - 1, here, :]
+            for a in range(count):
+                r = r0 + a
+                above = ref[r + 1, mid, :]
+                high = E[h][r, here, :]
+                right = N[h][r, mid, :]
+                left = N[h][r, down, :]
+                near = (
+                    high * above
+                    + low * below
+                    + right * ref[r, up, :]
+                    + left * ref[r, down, :]
+                )
+                emit(r, t, centre, near, high + low + right + left)
+                below, centre, low = centre, above, high
 
     def set_weights(h):
         shunt = SHUNT * 4.0**h
@@ -320,30 +342,41 @@
 
         rows_loop(1, R[h] + 2 * H[h] + 1, fill, unroll=2)
 
+    def s_tile(h, r, t):
+        here = pl.ds(8 * t, 8)
+        return s0[r - 1, here, :] if h == 0 else S[h][r, here, :]
+
     def presmooth(h):
         lo = 1 if h == 0 else 2
 
-        def fill(r):
-            V[h][r, win(h), :] = W[h][r] * (1.2 * s_row(h, r) + around_sum(h, U[h], r))
-
-        rows_loop(lo, R[h] + 2 * H[h] + 2 - lo, fill, unroll=2)
+        def emit(r, t, centre, near, total):
+            V[h][r, pl.ds(MARGIN + 8 * t, 8), :] = W[h][r, pl.ds(8 * t, 8), :] * (
+                1.2 * s_tile(h, r, t) + near
+            )
+
+        stencil(h, U[h], lo, R[h] + 2 * H[h] + 2 - lo, emit)
 
     def restrict(h):
         shunt = SHUNT * 4.0**h
-
-        def residual(r):
-            return (
-                s_row(h, r)
-                + around_sum(h, V[h], r)
-                - diagonal(h, r, shunt) * V[h][r, win(h), :]
-            )
-
         base = H[h] + 1
-
-        def fill(q):
-            U[h][q, win(h), :] = residual(base + 2 * q) + residual(base + 2 * q + 1)
-
-        rows_loop(0, R[h + 1], fill, unroll=2)
+        block = min(8, R[h])
+
+        def pairs(q):
+            held = {}
+
+            def emit(r, t, centre, near, total):
+                value = s_tile(h, r, t) + near - (shunt + total) * centre
+                if t in held:
+                    first_r, first_value = held.pop(t)
+                    U[h][first_r, pl.ds(MARGIN + 8 * t, 8), :] = first_value + value
+                else:
+                    held[t] = (q * (block // 2) + pairs_done[t], value)
+                    pairs_done[t] += 1
+
+            pairs_done = {t: 0 for t in range(JP[h] // 8)}
+            stencil_rows(h, V[h], base + q * block, block, emit)
+
+        rows_loop(0, R[h] // block, pairs)
         cc = C[h + 1]
 
         def halve(q):
@@ -399,14 +432,18 @@
                             di, dd + REACH, pl.ds(base + lo - first_j, hi - lo), :
                         ]
 
-        def fill(i, di, shift):
-            r = i + H[h] + 1 + shift
-            E[h][r] = spread(CX[h][0, di, pl.ds(MARGIN, JP[h]), :], i, JP[h])
-            N[h][r] = spread(CX[h][1, di], i, width)
-
-        rows_loop(R[h] - H[h] - 1, R[h], functools.partial(fill, di=0, shift=-R[h]))
-        rows_loop(0, R[h], functools.partial(fill, di=1, shift=0), unroll=4)
-        rows_loop(0, H[h] + 1, functools.partial(fill, di=2, shift=R[h]))
+        for di, lo, hi in (
+            (0, R[h] - H[h] - 1, R[h]),
+            (1, 0, R[h]),
+            (2, 0, H[h] + 1),
+        ):
+            east = CX[h][0, di, pl.ds(MARGIN, JP[h]), :]
+            north = CX[h][1, di]
+            for i in range(lo, hi):
+                r = i + H[h] + 1 + (di - 1) * R[h]
+                E[h][r] = spread(east, i, JP[h])
+                N[h][r] = spread(north, i, width)
+
         set_weights(h)
 
     nb = n_dev
@@ -505,10 +542,10 @@
         restrict(h)
     src_near = gather_near(g_src)
     start(src_near)
-    eliminate(5)
     wait(src_near)
     src_far = gather_far(g_src)
     start(src_far)
+    eliminate(5)
     invert(PP[6])
     x_ext[...] = jnp.zeros_like(x_ext)
     wait(src_far)
@@ -539,16 +576,13 @@
         for i in range(12):
             c5[i, k : k + 1, :] = part[6 + i : 7 + i]
 
-    def smooth(h, dst, ref, halo):
-        lo = H[h] + 1 - halo if h else 1
-        hi = R[h] + H[h] + 1 + halo if h else n_rows + 1
-
-        def fill(r):
-            dst[r, win(h), :] = 0.2 * ref[r, win(h), :] + W[h][r] * (
-                s_row(h, r) + around_sum(h, ref, r)
+    def smooth(h, dst, ref, lo, hi):
+        def emit(r, t, centre, near, total):
+            dst[r, pl.ds(MARGIN + 8 * t, 8), :] = 0.2 * centre + W[h][r, pl.ds(8 * t, 8), :] * (
+                s_tile(h, r, t) + near
             )
 
-        rows_loop(lo, hi, fill, unroll=2)
+        stencil(h, ref, lo, hi, emit)
 
     for h in range(LEVELS - 1, 0, -1):
         p = H[h] - 1
@@ -568,8 +602,9 @@
                     V[h][r, cols, :] = V[h][r, cols, :] + coarse
 
         rows_loop(-first_q, R[h] // 2 + first_q, lift, unroll=2)
-        smooth(h, U[h], V[h], p - 1)
-        smooth(h, V[h], U[h], p - 2)
+        own = H[h] + 1
+        smooth(h, U[h], V[h], own - (p - 1), own + R[h] + (p - 1))
+        smooth(h, V[h], U[h], own - (p - 2), own + R[h] + (p - 2))
 
     half_cols = n_cols // 2
 
@@ -590,13 +625,7 @@
     cols = pl.ds(MARGIN, n_cols)
     for c in order:
         lo = 1 + c * size
-
-        def fill(r):
-            u0[r, win(0), :] = 0.2 * v0[r, win(0), :] + W[0][r] * (
-                s0[r - 1] + around_sum(0, v0, r)
-            )
-
-        rows_loop(lo, lo + size, fill, unroll=2)
+        smooth(0, u0, v0, lo, lo + size)
         rows = pl.ds(lo, size)
         mine = [
             remote(u0.at[rows, pl.ds(MARGIN + n_cols - 1, 1), :], u0.at[rows, pl.ds(MARGIN - 1, 1), :], at(0, 1)),
@@ -618,12 +647,11 @@
         if c == 0:
             last_row.wait()
 
-        def last(r):
-            s0[r - 1] = 0.2 * u0[r, win(0), :] + W[0][r] * (
-                s0[r - 1] + around_sum(0, u0, r)
-            )
-
-        rows_loop(1 + c * size, 1 + c * size + size, last, unroll=2)
+        def last(r, t, centre, near, total):
+            here = pl.ds(8 * t, 8)
+            s0[r - 1, here, :] = 0.2 * centre + w0[r, here, :] * (s0[r - 1, here, :] + near)
+
+        stencil(0, u0, 1 + c * size, 1 + c * size + size, last)
         rows = pl.ds(c * size, size)
         done.append(pltpu.make_async_copy(s0.at[rows], out_hbm.at[rows], local.at[2 + c]))
         done[-1].start()
@@ -668,7 +696,7 @@
     scratch = [
         vm(n_rows, n_cols, LANES), vm(*ext0), vm(*ext0),
         vm(n_rows + 1, n_cols, LANES), vm(n_rows + 1, n_cols + MARGIN, LANES),
-        vm(n_rows + 1, n_cols, LANES), vm(n_cols + MARGIN, n_rows),
+        vm(n_rows + 1, n_cols, LANES), vm(n_cols, n_rows), vm(n_cols + MARGIN, n_rows),
         vm(3, 2 * REACH + 1, PACK_ROWS, LANES),
     ]
     scratch += [vm(tall[h], WIDTH[h], LANES) for h in levels]

time: 125 us -> 107 us (0.86)
  Pallas kernels: 119 us -> 102 us
    pallas_call x1, Pallas kernels: 114 us -> 95.1 us  [body(): pl.pallas_call(functools.partial(cycle_kernel, n_grp, n_dev, n_rows, n_co...]
where the time goes in v3:
time: 107 us; the launch traced here: 106 us
  Pallas kernels  102 us (95%)
  local copies, waits for them, and re-layouts  4.64 us (4%)
    pallas_call x1, Pallas kernels, body(): pl.pallas_call(functools.partial(cycle_kernel, n_grp, n_dev, n_rows, n_co...  95.1 us
    pallas_call x1, Pallas kernels, body(): pl.pallas_call(functools.partial(tap_kernel, n_rows, n_cols, total.bit_le...  6.4 us
    unnamed x1, local copies, waits for them, and re-layouts  4.64 us

profile of v3, /device:TPU:1, one launch (start us, length us, event | category | flops | bytes accessed | tf_op | source)
XLA Modules:
  0.0 106.2 jit_solution(4819077832521411956)
XLA Ops:
  0.0 6.4 %shard_map.64 = (f32[288,32,128]{2,1,0:T(8,128)}, s32[256]{0:T(256)}) custom-call(s32[16,128]{1,0:T(8,128)} %bitcast.6, f32[16,128]{1,0:T(8,128)} %bitcast.7), custom_call_target="tpu_custom_call" | custom-call | tf_op jit(solution)/shard_map/pallas_call | solution.py:671
  6.4 95.1 %shard_map.65 = f32[256,32,128]{2,1,0:T(8,128)} custom-call(f32[256,32,128]{2,1,0:T(8,128)} %load_hbm.1, f32[288,32,128]{2,1,0:T(8,128)} %get-tuple-element.7.table_hbm, s32[256]{0:T(256)} %get-tuple-element.8.slot_ref, s32[32,256]{1,0:T(8,128)} %bitcast.4, s32[32,256]{1,0:T(8,128)} %bitcast.5, f32[8]{0:T(128)} %tab_ref.1), custom_call_target="tpu_custom_call" | custom-call | tf_op jit(solution)/shard_map/pallas_call | solution.py:718
  101.5 4.6 %copy.8 = f32[256,32,128]{2,1,0:T(8,128)} copy(f32[256,32,128]{2,1,0:T(8,128)} %shard_map.65) | data formatting | bytes 8388608

commit v4 on v3

--- a/solution.py
+++ b/solution.py
@@ -15,9 +15,12 @@
 RELAX = 0.8
 LANES = 128
 
-HALO = {1: 4, 2: 5, 3: 5, 4: 5}
-WIDTH = {1: 24, 2: 24, 3: 16, 4: 16}
-OFFSET = {1: 4, 2: 8, 3: 6, 4: 6}
+HALO = {1: 6, 2: 5, 3: 6, 4: 5}
+WIDTH = {1: 32, 2: 24, 3: 24, 4: 16}
+OFFSET = {1: 7, 2: 8, 3: 7, 4: 6}
+UPWARD = {1: 3, 2: 4, 3: 4, 4: 4}
+DOWNWARD = {0: 0, 1: 6, 2: 2, 3: 6, 4: 2}
+GROW = {0: 0, 1: 2, 2: 0, 3: 2, 4: 0}
 PACK_E = {1: 0, 2: 32, 3: 48, 4: 56}
 PACK_N = {1: 16, 2: 40, 3: 52, 4: 58}
 PACK_ROWS = 64
@@ -59,21 +62,25 @@
     lax.fori_loop(0, n_rows, clear, 0, unroll=8)
     table[0] = jnp.zeros((n_cols, LANES), F32)
 
+    lower = jnp.where(inside, rows, -1)
+
     def more(carry):
-        return carry[1] < far
-
-    def one(carry):
-        used, row = carry
-        following = jnp.min(jnp.where(rows > row, rows, far))
-        here = jnp.where(rows == row, cur, 0.0)
-        total = jnp.zeros((n_cols, LANES), F32)
-        for k in range(taps.shape[0]):
-            total += jnp.where(cols[k : k + 1] == col_ids, here[k : k + 1], 0.0)
-        table[used] = total
-        slot_ref[row] = used
-        return used + 1, following
-
-    used, _ = lax.while_loop(more, one, (jnp.int32(1), jnp.min(rows)))
+        return carry[1] <= carry[2]
+
+    def two(carry):
+        used, low, high = carry
+        after = jnp.min(jnp.where(rows > low, rows, far))
+        before = jnp.max(jnp.where(lower < high, lower, -1))
+        for step, row in enumerate((low, high)):
+            here = jnp.where(rows == row, cur, 0.0)
+            total = jnp.zeros((n_cols, LANES), F32)
+            for k in range(taps.shape[0]):
+                total += jnp.where(cols[k : k + 1] == col_ids, here[k : k + 1], 0.0)
+            table[used + step] = total
+            slot_ref[row] = used + step
+        return used + 2, after, before
+
+    used, _, _ = lax.while_loop(more, two, (jnp.int32(1), jnp.min(rows), jnp.max(lower)))
 
     def part(c):
         at = pl.ds(c * TABLE_PART, TABLE_PART)
@@ -114,10 +121,10 @@
     s0, u0, v0, e0, n0, w0, et_ref, nt_ext, pack,
     s1, s2, s3, s4, u1, u2, u3, u4, v1, v2, v3, v4,
     e1, e2, e3, e4, n1, n2, n3, n4, w1, w2, w3, w4,
-    cx1, cx2, cx3, cx4,
+    cx1, cx2, cx3, cx4, sx2, sx4,
     g_cond, g_src, x_ext, c5,
     m1, m2, m3, m4, m5, y1, y2, y3, y4, y5, t1, t2, t3, t4, t5, p1, p2, p3, p4, p5, p6,
-    send, recv, local,
+    send, recv, local, own_sem,
 ):
     g = lax.axis_index("grp")
     d = lax.axis_index("dev")
@@ -129,6 +136,8 @@
     W = {0: w0, 1: w1, 2: w2, 3: w3, 4: w4}
     CX = {1: cx1, 2: cx2, 3: cx3, 4: cx4}
     S[0] = s0
+    SX = {0: s0, 1: s1, 2: sx2, 3: s3, 4: sx4}
+    BASE = {0: MARGIN, 1: 0, 2: 0, 3: 0, 4: 0}
     MT = {1: m1, 2: m2, 3: m3, 4: m4, 5: m5}
     YY = {1: y1, 2: y2, 3: y3, 4: y4, 5: y5}
     YT = {1: t1, 2: t2, 3: t3, 4: t4, 5: t5}
@@ -225,6 +234,22 @@
     mine8 = pl.ds(pl.multiple_of(g * 8, 8), 8)
     g_cond[d, mine8, :] = both
 
+    def spread(block, lane, width):
+        return jnp.broadcast_to(block[:, lane : lane + 1], (width, LANES))
+
+    et_ref[...] = et
+
+    def spread_part(dst, src, first_row, width):
+        def fill(half):
+            base = pl.multiple_of(half * LANES, LANES)
+            blk = src[first_row : first_row + width, pl.ds(base, LANES)]
+            for i in range(LANES):
+                dst[base + i + 1, pl.ds(first_row, width), :] = spread(blk, i, width)
+
+        rows_loop(0, n_rows // LANES, fill)
+
+    spread_part(e0, et_ref, 0, n_cols)
+    spread_part(n0, nt_ext, MARGIN, n_cols)
     pl.semaphore_wait(barrier, len(partners))
 
     def gather_near(buf):
@@ -247,7 +272,9 @@
     north_edge = [
         remote(nt_ext.at[pl.ds(MARGIN + n_cols - 1, 1), :], nt_ext.at[pl.ds(MARGIN - 1, 1), :], at(0, 1))
     ]
+    east_edge = [remote(e0.at[n_rows], e0.at[0], at(1, 0))]
     start(north_edge)
+    start(east_edge)
     cond_near = gather_near(g_cond)
     start(cond_near)
     pack_copies = []
@@ -259,25 +286,8 @@
         )
     start(pack_copies)
 
-    def spread(block, lane, width):
-        return jnp.broadcast_to(block[:, lane : lane + 1], (width, LANES))
-
-    et_ref[...] = et
-
-    def spread_part(dst, src, width):
-        def fill(half):
-            base = pl.multiple_of(half * LANES, LANES)
-            blk = src[:, pl.ds(base, LANES)]
-            for i in range(LANES):
-                dst[base + i + 1] = spread(blk, i, width)
-
-        rows_loop(0, n_rows // LANES, fill)
-
-    spread_part(e0, et_ref, n_cols)
-    east_edge = [remote(e0.at[n_rows], e0.at[0], at(1, 0))]
-    start(east_edge)
     wait(north_edge)
-    spread_part(n0, nt_ext, n_cols + MARGIN)
+    spread_part(n0, nt_ext, 0, MARGIN)
 
     wait(cond_near)
     cond_far = gather_far(g_cond)
@@ -285,10 +295,12 @@
     wait(east_edge)
 
     def win(h, shift=0):
-        return pl.ds(MARGIN + shift, JP[h])
+        return pl.ds(BASE[h] + shift, JP[h])
 
     def diagonal(h, r, shunt):
-        return shunt + E[h][r] + E[h][r - 1] + N[h][r, win(h), :] + N[h][r, win(h, -1), :]
+        right = N[h][r, win(h), :]
+        left = N[h][r, win(h, -1), :] if h == 0 else pltpu.roll(right, 1, 0)
+        return shunt + E[h][r] + E[h][r - 1] + right + left
 
     def stencil(h, ref, lo, hi, emit, block=8):
         def some(r0, count):
@@ -300,11 +312,10 @@
             some(lo + full * block, hi - lo - full * block)
 
     def stencil_rows(h, ref, r0, count, emit):
-        for t in range(JP[h] // 8):
+        tiles = JP[h] // 8
+        for t in range(tiles):
             here = pl.ds(8 * t, 8)
-            mid = pl.ds(MARGIN + 8 * t, 8)
-            up = pl.ds(MARGIN + 8 * t + 1, 8)
-            down = pl.ds(MARGIN + 8 * t - 1, 8)
+            mid = pl.ds(BASE[h] + 8 * t, 8)
             below = ref[r0 - 1, mid, :]
             centre = ref[r0, mid, :]
             low = E[h][r0 - 1, here, :]
@@ -313,13 +324,17 @@
                 above = ref[r + 1, mid, :]
                 high = E[h][r, here, :]
                 right = N[h][r, mid, :]
-                left = N[h][r, down, :]
-                near = (
-                    high * above
-                    + low * below
-                    + right * ref[r, up, :]
-                    + left * ref[r, down, :]
-                )
+                if h == 0 or t < tiles - 1:
+                    after = ref[r, pl.ds(BASE[h] + 8 * t + 1, 8), :]
+                else:
+                    after = pltpu.roll(centre, 7, 0)
+                if h == 0 or t > 0:
+                    before = ref[r, pl.ds(BASE[h] + 8 * t - 1, 8), :]
+                    left = N[h][r, pl.ds(BASE[h] + 8 * t - 1, 8), :]
+                else:
+                    before = pltpu.roll(centre, 1, 0)
+                    left = pltpu.roll(right, 1, 0)
+                near = high * above + low * below + right * after + left * before
                 emit(r, t, centre, near, high + low + right + left)
                 below, centre, low = centre, above, high
 
@@ -331,63 +346,69 @@
 
         rows_loop(1, R[h] + 2 * H[h] + 1, fill, unroll=2)
 
-    def s_row(h, r):
-        return s0[r - 1] if h == 0 else S[h][r]
-
-    def first(h):
+    def first(h, source=None, halo=None):
+        halo = DOWNWARD[h] if halo is None else halo
+        own = H[h] + 1
+
         def fill(r):
             if h == 0:
                 s0[r - 1] = v0[slot_ref[r - 1], win(0), :] - s0[r - 1]
-            U[h][r, win(h), :] = W[h][r] * s_row(h, r)
-
-        rows_loop(1, R[h] + 2 * H[h] + 1, fill, unroll=2)
-
-    def s_tile(h, r, t):
+                U[0][r, win(0), :] = W[0][r] * s0[r - 1]
+            else:
+                U[h][r] = W[h][r] * (S[h] if source is None else source)[r]
+
+        rows_loop(own - halo, own + R[h] + halo, fill, unroll=2)
+
+    def s_tile(h, r, t, source=None):
         here = pl.ds(8 * t, 8)
-        return s0[r - 1, here, :] if h == 0 else S[h][r, here, :]
-
-    def presmooth(h):
-        lo = 1 if h == 0 else 2
+        return s0[r - 1, here, :] if h == 0 else (S[h] if source is None else source)[r, here, :]
+
+    def presmooth(h, source=None, halo=None):
+        halo = max(DOWNWARD[h] - 1, 0) if halo is None else halo
+        own = H[h] + 1
 
         def emit(r, t, centre, near, total):
-            V[h][r, pl.ds(MARGIN + 8 * t, 8), :] = W[h][r, pl.ds(8 * t, 8), :] * (
-                1.2 * s_tile(h, r, t) + near
+            V[h][r, pl.ds(BASE[h] + 8 * t, 8), :] = W[h][r, pl.ds(8 * t, 8), :] * (
+                1.2 * s_tile(h, r, t, source) + near
             )
 
-        stencil(h, U[h], lo, R[h] + 2 * H[h] + 2 - lo, emit)
+        stencil(h, U[h], own - halo, own + R[h] + halo, emit)
 
     def restrict(h):
         shunt = SHUNT * 4.0**h
-        base = H[h] + 1
-        block = min(8, R[h])
+        grow = GROW[h]
+        base = H[h] + 1 - 2 * grow
+        count = R[h] + 4 * grow
+        block = 8
 
         def pairs(q):
             held = {}
+            pairs_done = {t: 0 for t in range(JP[h] // 8)}
 
             def emit(r, t, centre, near, total):
                 value = s_tile(h, r, t) + near - (shunt + total) * centre
                 if t in held:
                     first_r, first_value = held.pop(t)
-                    U[h][first_r, pl.ds(MARGIN + 8 * t, 8), :] = first_value + value
+                    U[h][first_r, pl.ds(BASE[h] + 8 * t, 8), :] = first_value + value
                 else:
                     held[t] = (q * (block // 2) + pairs_done[t], value)
                     pairs_done[t] += 1
 
-            pairs_done = {t: 0 for t in range(JP[h] // 8)}
             stencil_rows(h, V[h], base + q * block, block, emit)
 
-        rows_loop(0, R[h] // block, pairs)
-        cc = C[h + 1]
+        rows_loop(0, count // block, pairs)
+        cc = C[h + 1] + 2 * grow
+        from_col = BASE[h] + OJ[h] - 2 * grow
 
         def halve(q):
-            a = U[h][q, pl.ds(MARGIN + OJ[h], cc, stride=2), :]
-            b = U[h][q, pl.ds(MARGIN + OJ[h] + 1, cc, stride=2), :]
+            a = U[h][q, pl.ds(from_col, cc, stride=2), :]
+            b = U[h][q, pl.ds(from_col + 1, cc, stride=2), :]
             if h == LEVELS - 1:
                 g_src[d, pl.ds(g * 8 + q, 1), :] = a + b
             else:
-                S[h + 1][q + H[h + 1] + 1, pl.ds(OJ[h + 1], cc), :] = a + b
-
-        rows_loop(0, R[h + 1], halve, unroll=2)
+                S[h + 1][q - grow + H[h + 1] + 1, pl.ds(OJ[h + 1] - grow, cc), :] = a + b
+
+        rows_loop(0, count // 2, halve, unroll=2)
 
     def edges(ref):
         rows = pl.ds(1, n_rows)
@@ -406,10 +427,15 @@
             i0, ni = overlap(di, R[h], H[h])
             j0, nj = overlap(dd, C[h], H[h])
             src = S[h].at[pl.ds(i0 + H[h] + 1, ni), pl.ds(j0 + OJ[h], nj), :]
-            dst = S[h].at[
+            dst = SX[h].at[
                 pl.ds(i0 - di * R[h] + H[h] + 1, ni), pl.ds(j0 - dd * C[h] + OJ[h], nj), :
             ]
             copies.append(remote(src, dst, at(di, dd)))
+        if SX[h] is not S[h]:
+            own = (pl.ds(H[h] + 1, R[h]), pl.ds(OJ[h], C[h]))
+            copies.append(
+                pltpu.make_async_copy(S[h].at[own[0], own[1], :], SX[h].at[own[0], own[1], :], own_sem.at[h])
+            )
         return copies
 
     set_weights(0)
@@ -420,12 +446,12 @@
     start(u_edges)
 
     def spread_level(h):
-        width = MARGIN + JP[h]
+        width = JP[h]
         for t, base in ((0, PACK_E[h]), (1, PACK_N[h])):
             for di in range(3):
                 for dd in range(-REACH, REACH + 1):
-                    first_j = dd * C[h] + OJ[h] + MARGIN
-                    lo = max(first_j, MARGIN - 1)
+                    first_j = dd * C[h] + OJ[h]
+                    lo = max(first_j, 0)
                     hi = min(first_j + C[h], width)
                     if hi > lo and abs(dd) <= -(-(H[h] + 1) // C[h]):
                         CX[h][t, di, pl.ds(lo, hi - lo), :] = pack[
@@ -437,7 +463,7 @@
             (1, 0, R[h]),
             (2, 0, H[h] + 1),
         ):
-            east = CX[h][0, di, pl.ds(MARGIN, JP[h]), :]
+            east = CX[h][0, di]
             north = CX[h][1, di]
             for i in range(lo, hi):
                 r = i + H[h] + 1 + (di - 1) * R[h]
@@ -464,23 +490,56 @@
         block = jnp.where(lane == sub - 1, -low, block)
         return block, jnp.where(eye, -nc, 0.0), jnp.where(eye, -before, 0.0)
 
+    def inverse2(a, b, c, e):
+        t = 1.0 / (a * e - b * c)
+        return ((e * t, -b * t), (-c * t, a * t))
+
+    def times(m, v):
+        return [m[0][0] * v[0] + m[0][1] * v[1], m[1][0] * v[0] + m[1][1] * v[1]]
+
+    def product(m, o):
+        return [[m[i][0] * o[0][j] + m[i][1] * o[1][j] for j in range(2)] for i in range(2)]
+
     def invert(ref):
         count = ref.shape[0]
-        l3 = iota((count, nn, nn), 2)
-        s3_ = iota((count, nn, nn), 1)
-        lr = iota((count, 1, nn), 2)
-
-        def step(k, carry):
+        width = 2 if count > 8 else 4
+        l3 = iota((1, nn, nn), 2)
+        s3_ = iota((1, nn, nn), 1)
+        lr = iota((1, 1, nn), 2)
+        for k in range(0, nn, width):
             mat = ref[...]
-            row = ref[:, pl.ds(k, 1), :]
-            pivot = 1.0 / jnp.sum(jnp.where(lr == k, row, 0.0), axis=2, keepdims=True)
-            col = jnp.sum(jnp.where(l3 == k, mat, 0.0), axis=2, keepdims=True)
-            col = jnp.where(s3_ == k, -1.0, col)
-            row = jnp.where(lr == k, pivot, row * pivot)
-            ref[...] = jnp.where((l3 == k) | (s3_ == k), 0.0, mat) - col * row
-            return carry
-
-        lax.fori_loop(0, nn, step, 0)
+            cols = [
+                jnp.broadcast_to(mat[:, :, k + i : k + i + 1], (count, nn, nn)) for i in range(width)
+            ]
+            piv = [[cols[j][:, k + i : k + i + 1, :] for j in range(width)] for i in range(width)]
+            rows = []
+            for i in range(width):
+                row = mat[:, k + i : k + i + 1, :]
+                for j in range(width):
+                    row = jnp.where(lr == k + j, 1.0 if i == j else 0.0, row)
+                rows.append(row)
+            head = inverse2(piv[0][0], piv[0][1], piv[1][0], piv[1][1])
+            if width == 2:
+                rows = times(head, rows)
+            else:
+                right = [piv[0][2:], piv[1][2:]]
+                below = [piv[2][:2], piv[3][:2]]
+                carried = product(below, head)
+                fill = product(carried, right)
+                tail = inverse2(
+                    piv[2][2] - fill[0][0], piv[2][3] - fill[0][1],
+                    piv[3][2] - fill[1][0], piv[3][3] - fill[1][1],
+                )
+                y = times(carried, rows[:2])
+                low = times(tail, [rows[2] - y[0], rows[3] - y[1]])
+                y = times(right, low)
+                rows = times(head, [rows[0] - y[0], rows[1] - y[1]]) + low
+            inside = (s3_ >= k) & (s3_ < k + width)
+            new = jnp.where(inside | ((l3 >= k) & (l3 < k + width)), 0.0, mat)
+            for i in range(width):
+                col = jnp.where(inside, jnp.where(s3_ == k + i, -1.0, 0.0), cols[i])
+                new = new - col * rows[i]
+            ref[...] = new
 
     even = {}
 
@@ -521,33 +580,51 @@
             even[lev + 1] = new[0::2]
 
     wait(pack_copies)
-    spread_level(1)
+    for h in range(1, LEVELS):
+        spread_level(h)
     wait(u_edges)
     presmooth(0)
     v_edges = edges(v0)
     start(v_edges)
-    for h in range(2, LEVELS):
-        spread_level(h)
     wait(cond_far)
     matrices()
+    eliminate(1)
     wait(v_edges)
     restrict(0)
-    for h in range(1, LEVELS):
-        copies = halos(h)
-        start(copies)
-        eliminate(h)
-        wait(copies)
+    def down(h):
         first(h)
         presmooth(h)
         restrict(h)
+
+    copies = halos(1)
+    start(copies)
+    eliminate(2)
+    eliminate(3)
+    wait(copies)
+    down(1)
+    down(2)
+    copies = halos(3)
+    start(copies)
+    eliminate(4)
+    eliminate(5)
+    wait(copies)
+    late = halos(2)
+    start(late)
+    down(3)
+    down(4)
     src_near = gather_near(g_src)
     start(src_near)
+    more = halos(4)
+    start(more)
+    invert(PP[6])
     wait(src_near)
     src_far = gather_far(g_src)
     start(src_far)
-    eliminate(5)
-    invert(PP[6])
     x_ext[...] = jnp.zeros_like(x_ext)
+    for h, copies in ((2, late), (4, more)):
+        wait(copies)
+        first(h, SX[h], UPWARD[h] + 1)
+        presmooth(h, SX[h], UPWARD[h])
     wait(src_far)
 
     for lev in range(1, 6):
@@ -578,27 +655,28 @@
 
     def smooth(h, dst, ref, lo, hi):
         def emit(r, t, centre, near, total):
-            dst[r, pl.ds(MARGIN + 8 * t, 8), :] = 0.2 * centre + W[h][r, pl.ds(8 * t, 8), :] * (
-                s_tile(h, r, t) + near
+            dst[r, pl.ds(BASE[h] + 8 * t, 8), :] = 0.2 * centre + W[h][r, pl.ds(8 * t, 8), :] * (
+                s_tile(h, r, t, SX[h]) + near
             )
 
         stencil(h, ref, lo, hi, emit)
 
     for h in range(LEVELS - 1, 0, -1):
-        p = H[h] - 1
+        p = UPWARD[h]
         first_q = -(-p // 2)
-        size = JP[h] // 2
-
-        def lift(q, h=h, size=size):
+        odd_col = OJ[h] % 2
+        size = (JP[h] - odd_col) // 2
+
+        def lift(q, h=h, size=size, odd_col=odd_col):
             if h == LEVELS - 1:
                 coarse = c5[q + 2]
             else:
-                cofs = MARGIN + OJ[h + 1] - OJ[h] // 2
+                cofs = OJ[h + 1] - OJ[h] // 2
                 coarse = V[h + 1][q + H[h + 1] + 1, pl.ds(cofs, size), :]
             for a in range(2):
                 r = 2 * q + a + H[h] + 1
                 for b in range(2):
-                    cols = pl.ds(MARGIN + b, size, stride=2)
+                    cols = pl.ds(odd_col + b, size, stride=2)
                     V[h][r, cols, :] = V[h][r, cols, :] + coarse
 
         rows_loop(-first_q, R[h] // 2 + first_q, lift, unroll=2)
@@ -609,7 +687,7 @@
     half_cols = n_cols // 2
 
     def lift0(q, rows):
-        coarse = V[1][q + H[1] + 1, pl.ds(MARGIN + OJ[1] - 1, half_cols + 2), :]
+        coarse = V[1][q + H[1] + 1, pl.ds(OJ[1] - 1, half_cols + 2), :]
         for a in rows:
             r = 2 * q + a + 1
             for b in range(2):
@@ -700,11 +778,12 @@
         vm(3, 2 * REACH + 1, PACK_ROWS, LANES),
     ]
     scratch += [vm(tall[h], WIDTH[h], LANES) for h in levels]
-    scratch += [vm(tall[h], WIDTH[h] + 2 * MARGIN, LANES) for h in levels] * 2
+    scratch += [vm(tall[h], WIDTH[h], LANES) for h in levels] * 2
     scratch += [vm(tall[h], WIDTH[h], LANES) for h in levels]
-    scratch += [vm(tall[h], WIDTH[h] + MARGIN, LANES) for h in levels]
     scratch += [vm(tall[h], WIDTH[h], LANES) for h in levels]
-    scratch += [vm(2, 3, WIDTH[h] + MARGIN, LANES) for h in levels]
+    scratch += [vm(tall[h], WIDTH[h], LANES) for h in levels]
+    scratch += [vm(2, 3, WIDTH[h], LANES) for h in levels]
+    scratch += [vm(tall[h], WIDTH[h], LANES) for h in (2, 4)]
     scratch += [vm(n_dev, 32, LANES), vm(n_dev, 32, LANES), vm(n_dev + 8, 32 + 16, LANES), vm(12, 8, LANES)]
     scratch += [vm(nn >> l, 64, 32) for l in range(1, 6)]
     scratch += [vm(nn >> l, 32, 64) for l in range(1, 6)]
@@ -714,6 +793,7 @@
         pltpu.SemaphoreType.DMA((N_COPIES,)),
         pltpu.SemaphoreType.DMA((N_COPIES,)),
         pltpu.SemaphoreType.DMA((2 + PARTS,)),
+        pltpu.SemaphoreType.DMA((LEVELS,)),
     ]
     return pl.pallas_call(
         functools.partial(cycle_kernel, n_grp, n_dev, n_rows, n_cols),

time: 107 us -> 103 us (0.963)
  Pallas kernels: 102 us -> 97.9 us
    pallas_call x1, Pallas kernels: 95.1 us -> 92.8 us  [body(): pl.pallas_call(functools.partial(cycle_kernel, n_grp, n_dev, n_rows, n_co...]
    pallas_call x1, Pallas kernels: 6.4 us -> 5.11 us  [body(): pl.pallas_call(functools.partial(tap_kernel, n_rows, n_cols, total.bit_le...]
where the time goes in v4:
time: 103 us
  Pallas kernels  97.9 us (95%)
  local copies, waits for them, and re-layouts  4.64 us (5%)
    pallas_call x1, Pallas kernels, body(): pl.pallas_call(functools.partial(cycle_kernel, n_grp, n_dev, n_rows, n_co...  92.8 us
    pallas_call x1, Pallas kernels, body(): pl.pallas_call(functools.partial(tap_kernel, n_rows, n_cols, total.bit_le...  5.11 us
    unnamed x1, local copies, waits for them, and re-layouts  4.64 us

profile of v4, /device:TPU:1, one launch (start us, length us, event | category | flops | bytes accessed | tf_op | source)
XLA Modules:
  0.0 102.5 jit_solution(3683715139789982681)
XLA Ops:
  0.0 5.1 %shard_map.64 = (f32[288,32,128]{2,1,0:T(8,128)}, s32[256]{0:T(256)}) custom-call(s32[16,128]{1,0:T(8,128)} %bitcast.6, f32[16,128]{1,0:T(8,128)} %bitcast.7), custom_call_target="tpu_custom_call" | custom-call | tf_op jit(solution)/shard_map/pallas_call | solution.py:749
  5.1 92.8 %shard_map.65 = f32[256,32,128]{2,1,0:T(8,128)} custom-call(f32[256,32,128]{2,1,0:T(8,128)} %load_hbm.1, f32[288,32,128]{2,1,0:T(8,128)} %get-tuple-element.7.table_hbm, s32[256]{0:T(256)} %get-tuple-element.8.slot_ref, s32[32,256]{1,0:T(8,128)} %bitcast.4, s32[32,256]{1,0:T(8,128)} %bitcast.5, f32[8]{0:T(128)} %tab_ref.1), custom_call_target="tpu_custom_call" | custom-call | tf_op jit(solution)/shard_map/pallas_call | solution.py:798
  97.9 4.6 %copy.8 = f32[256,32,128]{2,1,0:T(8,128)} copy(f32[256,32,128]{2,1,0:T(8,128)} %shard_map.65) | data formatting | bytes 8388608

commit v5 on v4

--- a/solution.py
+++ b/solution.py
@@ -97,6 +97,24 @@
         @pl.when(used > c * TABLE_PART)
         def _():
             part(c).wait()
+
+
+def copy_kernel(parts, src, dst, buf, sems):
+    size = src.shape[0] // parts
+    rows = [pl.ds(i * size, size) for i in range(parts)]
+    reads = [
+        pltpu.make_async_copy(src.at[r], buf.at[r], sems.at[i]) for i, r in enumerate(rows)
+    ]
+    writes = [
+        pltpu.make_async_copy(buf.at[r], dst.at[r], sems.at[parts + i]) for i, r in enumerate(rows)
+    ]
+    for c in reads:
+        c.start()
+    for c, w in zip(reads, writes):
+        c.wait()
+        w.start()
+    for w in writes:
+        w.wait()
 
 
 def around(dist):
@@ -795,7 +813,7 @@
         pltpu.SemaphoreType.DMA((2 + PARTS,)),
         pltpu.SemaphoreType.DMA((LEVELS,)),
     ]
-    return pl.pallas_call(
+    result = pl.pallas_call(
         functools.partial(cycle_kernel, n_grp, n_dev, n_rows, n_cols),
         out_shape=jax.ShapeDtypeStruct(load.shape, F32),
         in_specs=[
@@ -812,6 +830,18 @@
             collective_id=0, has_side_effects=True, vmem_limit_bytes=63 << 20
         ),
     )(load, table, slot, east_class.T, north_class.T, cond_table)
+    parts = 4
+    return pl.pallas_call(
+        functools.partial(copy_kernel, parts),
+        out_shape=jax.ShapeDtypeStruct(load.shape, F32),
+        in_specs=[pl.BlockSpec(memory_space=pl.ANY)],
+        out_specs=pl.BlockSpec(memory_space=pl.ANY),
+        scratch_shapes=[
+            vm(n_rows, n_cols, LANES),
+            pltpu.SemaphoreType.DMA((2 * parts,)),
+        ],
+        compiler_params=pltpu.CompilerParams(vmem_limit_bytes=60 << 20),
+    )(result)
 
 
 def solution(mesh):

time: 103 us -> 102 us (level)
  local copies, waits for them, and re-layouts: 4.64 us -> 0 us
  Pallas kernels: 97.9 us -> 102 us
    unnamed x1 -> x0, local copies, waits for them, and re-layouts: 4.64 us -> none
    pallas_call x0 -> x1, Pallas kernels: none -> 3.3 us  [body(): pl.pallas_call(functools.partial(copy_kernel, parts), out_shape=jax.Shape...]
where the time goes in v5:
time: 102 us
  Pallas kernels  102 us (100%)
    pallas_call x1, Pallas kernels, body(): pl.pallas_call(functools.partial(cycle_kernel, n_grp, n_dev, n_rows, n_co...  93.5 us
    pallas_call x1, Pallas kernels, body(): pl.pallas_call(functools.partial(tap_kernel, n_rows, n_cols, total.bit_le...  4.87 us
    pallas_call x1, Pallas kernels, body(): pl.pallas_call(functools.partial(copy_kernel, parts), out_shape=jax.Shape...  3.3 us

profile of v5, /device:TPU:1, one launch (start us, length us, event | category | flops | bytes accessed | tf_op | source)
XLA Modules:
  0.0 101.8 jit_solution(1553178453020095350)
XLA Ops:
  0.0 4.9 %shard_map.64 = (f32[288,32,128]{2,1,0:T(8,128)}, s32[256]{0:T(256)}) custom-call(s32[16,128]{1,0:T(8,128)} %bitcast.6, f32[16,128]{1,0:T(8,128)} %bitcast.7), custom_call_target="tpu_custom_call" | custom-call | tf_op jit(solution)/shard_map/pallas_call | solution.py:767
  4.9 93.5 %shard_map.65.src = f32[256,32,128]{2,1,0:T(8,128)} custom-call(f32[256,32,128]{2,1,0:T(8,128)} %load_hbm.1, f32[288,32,128]{2,1,0:T(8,128)} %get-tuple-element.7.table_hbm, s32[256]{0:T(256)} %get-tuple-element.8.slot_ref, s32[32,256]{1,0:T(8,128)} %bitcast.4, s32[32,256]{1,0:T(8,128)} %bitcast.5, f32[8]{0:T(128)} %tab_ref.1), custom_call_target="tpu_custom_call" | custom-call | tf_op jit(solution)/shard_map/pallas_call | solution.py:816
  98.4 3.3 %shard_map.66 = f32[256,32,128]{2,1,0:T(8,128)} custom-call(f32[256,32,128]{2,1,0:T(8,128)} %shard_map.65.src), custom_call_target="tpu_custom_call" | custom-call | tf_op jit(solution)/shard_map/pallas_call | solution.py:834
